TPU v7x, 256 devices: a whole 4x4x8 slice. The times are simulated.
256 devices in a mesh: tm: 8 (over y, core), rows: 32 (over x, z).
Axes of the slice: x: 4, y: 4, z: 8, core: 2. Of those that a mesh axis runs over, the one named last changes fastest.
Arguments:
- latent: bfloat16 [8, 96, 128, 384], P('tm', 'rows'), may hold values from -6 to 6
- norm1_gain: float32 [384], replicated, may hold values from 0.1 to 1.9
- conv1_weight: bfloat16 [3, 3, 3, 384, 384], replicated, may hold values from -0.0625 to 0.0625
- conv1_bias: float32 [384], replicated, may hold values from -3 to 3
- attention_gain: float32 [384], replicated, may hold values from 0.1 to 1.9
- qkv_weight: bfloat16 [384, 1152], replicated, may hold values from -1.5 to 1.5
- qkv_bias: float32 [1152], replicated, may hold values from -28 to 28
- proj_weight: bfloat16 [384, 384], replicated, may hold values from -0.3125 to 0.3125
- proj_bias: float32 [384], replicated, may hold values from -3 to 3
- up_weight: bfloat16 [3, 3, 384, 192], replicated, may hold values from -0.109375 to 0.109375
- up_bias: float32 [192], replicated, may hold values from -3 to 3
Outputs:
- upsampled: bfloat16 [8, 192, 256, 192], P('tm', 'rows')
All inputs are finite; a program needn't handle non-finite values.
Results may differ from a plain program's by a relative error of at most 0.035.
Values may be sent and summed in bfloat16 or wider, within the bound.
No kernel may reach another device: no remote copies, remote signals or barrier semaphores. Data moves between devices by JAX's collectives and lax.ppermute only.
A program may use at most 128 MiB of HBM per device.

v0:
```python
import functools
import math

import jax
import jax.numpy as jnp
from jax import lax
from jax.experimental import pallas as pl
from jax.experimental.pallas import tpu as pltpu
from jax.sharding import PartitionSpec as P

F32 = jnp.float32
BF16 = jnp.bfloat16
ROWS = 3
W = 128
C = 384
OUT = 192
CELLS = ROWS * W
XN, ZN, TN = 4, 8, 8
QALL = XN * CELLS
HALF = C // 2
STAT = 16
LOG2E = math.log2(math.e)


def dot(a, b, dims):
    return lax.dot_general(a, b, (dims, ((), ())), preferred_element_type=F32)


def params(mib=32):
    return pltpu.CompilerParams(vmem_limit_bytes=mib * 2**20)


def cost(flops, bytes_accessed):
    return pl.CostEstimate(flops=int(flops), bytes_accessed=int(bytes_accessed), transcendentals=0)


VM = pl.BlockSpec(memory_space=pltpu.VMEM)
ANY = pl.BlockSpec(memory_space=pl.ANY)
HBM = pl.BlockSpec(memory_space=pltpu.HBM)


def call(body, outs, *args, name, flops=1e6, nbytes=1e6, aliases=None, scratch=(), mib=32, specs=None, out_spec=VM):
    shapes = [jax.ShapeDtypeStruct(shape, dtype) for shape, dtype in outs]
    result = pl.pallas_call(
        body,
        in_specs=specs or [VM] * len(args),
        out_specs=[out_spec] * len(shapes),
        out_shape=shapes,
        input_output_aliases=aliases or {},
        scratch_shapes=list(scratch),
        compiler_params=params(mib),
        cost_estimate=cost(flops, nbytes),
        name=name,
    )(*args)
    return result[0] if len(shapes) == 1 else result


def col_variants(y, store):
    column = lax.broadcasted_iota(jnp.int32, y.shape, 0)
    before = jnp.where(column == 0, 0.0, pltpu.roll(y, 1, 0))
    after = jnp.where(column == W - 1, 0.0, pltpu.roll(y, W - 1, 0))
    store(0, before.astype(BF16))
    store(1, y.astype(BF16))
    store(2, after.astype(BF16))


def activate(row, gain):
    x = row.astype(F32)
    y = x * lax.rsqrt(jnp.mean(x * x, -1, keepdims=True) + 1e-6) * gain
    y = y / (1.0 + jnp.exp(-y))
    return y.astype(BF16).astype(F32)


def inside():
    frame, band = lax.axis_index("tm"), lax.axis_index("rows")
    return frame >= 2, frame >= 1, band >= 1, band < XN * ZN - 1


def fill_rows(scratch, rows, gain, present=None):
    for index, row in enumerate(rows):
        y = activate(row, gain)
        if present is not None:
            y = jnp.where(present[index], y, 0.0)

        def store(variant, value, index=index):
            scratch[index, :, variant * C : (variant + 1) * C] = value

        col_variants(y, store)


def band_rows(scratch, t, frame, gain, present=None):
    zero = jnp.zeros((W, 3 * C), BF16)
    scratch[t, 0] = zero
    scratch[t, 1 + ROWS] = zero
    present = None if present is None else [present] * ROWS
    fill_rows(scratch.at[t, 1 : 1 + ROWS], [frame[i] for i in range(ROWS)], gain, present)


def band_tap(scratch, t, b, weight):
    left = scratch[t, pl.ds(b, ROWS)].reshape(CELLS, 3 * C)
    return dot(left, weight.reshape(3 * C, C), ((1,), (0,)))


def conv_own_kernel(own, small, weight, acc, beside, earlier, scratch, held, sem, rest_sem):
    def copy(b):
        return pltpu.make_async_copy(weight.at[2, b], held.at[b], sem.at[b])

    for b in range(3):
        copy(b).start()
    rest = [
        pltpu.make_async_copy(weight.at[2, 0], beside.at[0], rest_sem.at[0]),
        pltpu.make_async_copy(weight.at[2, 2], beside.at[1], rest_sem.at[1]),
        pltpu.make_async_copy(weight.at[:2], earlier, rest_sem.at[2]),
    ]
    for one in rest:
        one.start()
    band_rows(scratch, 0, own, small[0:1, :C])
    acc[...] = jnp.zeros((CELLS, C), F32)

    def step(b, carry):
        copy(b).wait()
        acc[...] += band_tap(scratch, 0, b, held[b])
        return carry

    lax.fori_loop(0, 3, step, 0)
    for one in rest:
        one.wait()


def conv_own(own, small, weight):
    return call(
        conv_own_kernel,
        [((CELLS, C), F32), ((2, 3, C, C), BF16), ((2, 3, 3, C, C), BF16)],
        own,
        small,
        weight,
        name="conv_own",
        flops=2 * CELLS * 9 * C * C,
        scratch=[
            pltpu.VMEM((1, ROWS + 2, W, 3 * C), BF16),
            pltpu.VMEM((3, 3, C, C), BF16),
            pltpu.SemaphoreType.DMA((3,)),
            pltpu.SemaphoreType.DMA((3,)),
        ],
        specs=[VM, VM, HBM],
        mib=46,
    )


def conv_earlier_kernel(two, one, small, weight, start, acc, scratch):
    has_two, has_one, _, _ = inside()
    band_rows(scratch, 0, two, small[0:1, :C], has_two)
    band_rows(scratch, 1, one, small[0:1, :C], has_one)
    acc[...] = start[...]

    def step(g, carry):
        t, b = g // 3, g % 3
        acc[...] += band_tap(scratch, t, b, weight[t, b])
        return carry

    lax.fori_loop(0, 6, step, 0)


def conv_earlier(two, one, small, weight, start):
    return call(
        conv_earlier_kernel,
        [((CELLS, C), F32)],
        two,
        one,
        small,
        weight,
        start,
        name="conv_earlier",
        flops=2 * CELLS * 18 * C * C,
        scratch=[pltpu.VMEM((2, ROWS + 2, W, 3 * C), BF16)],
        aliases={4: 0},
    )


def edge_taps(scratch, low, high, first, last):
    left = dot(scratch[low], first[...].reshape(3 * C, C), ((1,), (0,)))
    right = dot(scratch[high], last[...].reshape(3 * C, C), ((1,), (0,)))
    return left, right


def conv_edges_kernel(low, high, small, w_own, w_pair, start, acc, scratch):
    two, _, above, below = inside()
    present = [above, above & two, below, below & two]
    fill_rows(scratch, [low[0], low[1], high[0], high[1]], small[0:1, :C], present)
    own = edge_taps(scratch, 0, 2, w_own.at[0], w_own.at[1])
    two = edge_taps(scratch, 1, 3, w_pair.at[0, 0], w_pair.at[0, 2])
    acc[...] = start[...]
    acc[:W] += own[0] + two[0]
    acc[2 * W :] += own[1] + two[1]


def conv_last_kernel(edges, own, small, weight, start, block, normed, scratch):
    _, one, above, below = inside()
    fill_rows(scratch, [edges[0], edges[1]], small[0:1, :C], [above & one, below & one])
    sides = edge_taps(scratch, 0, 1, weight.at[1, 0], weight.at[1, 2])
    bias, gain2 = small[1:2, :C], small[2:3, :C]
    for i in range(ROWS):
        rows = slice(i * W, (i + 1) * W)
        total = start[rows] + bias
        if i != 1:
            total += sides[i // 2]
        x = (own[i].astype(F32) + total.astype(BF16).astype(F32)).astype(BF16)
        block[rows] = x
        x = x.astype(F32)
        x = x * lax.rsqrt(jnp.mean(x * x, -1, keepdims=True) + 1e-6) * gain2
        normed[rows] = x.astype(BF16)


def edge_payload_kernel(own, two, _acc, to_next, to_previous, pair):
    to_next[0] = own[ROWS - 1]
    to_next[1] = two[ROWS - 1]
    to_previous[0] = own[0]
    to_previous[1] = two[0]

    odd = lax.rem(lax.axis_index("tm"), 2)

    @pl.when(odd == 0)
    def _():
        pair[...] = own[...]

    @pl.when(odd == 1)
    def _():
        pair[...] = two[...]


def pair_edges_kernel(low, high, _acc, out):
    index = lax.rem(lax.axis_index("tm"), 2)
    out[0] = low[index]
    out[1] = high[index]


def query_kernel(normed, weight, small, out, shift):
    scale = C**-0.5 * LOG2E
    wq, wk = weight[:, :C], weight[:, C : 2 * C]
    q = (dot(normed[...], wq, ((1,), (0,))) + small[4:5, :C]).astype(BF16)
    out[...] = (dot(wk, q, ((1,), (1,))) * scale).astype(BF16)
    bk = jnp.broadcast_to(small[4:5, C : 2 * C], (8, C))
    shift[...] = dot(bk, q.astype(F32), ((1,), (1,)))[:1] * scale


def spans(refs, low, high):
    at = 0
    for ref in refs:
        n = ref.shape[1]
        first, last = max(low, at), min(high, at + n)
        if first < last:
            yield ref, first - at, last - at, first - low, last - low
        at += n


def read(refs, low, high):
    pieces = [ref[:, a:b] for ref, a, b, _, _ in spans(refs, low, high)]
    return pieces[0] if len(pieces) == 1 else jnp.concatenate(pieces, 1)


def write(refs, low, high, value):
    for ref, a, b, first, last in spans(refs, low, high):
        ref[:, a:b] = value[:, first:last]


def joined(refs):
    return refs[0][...] if len(refs) == 1 else jnp.concatenate([r[...] for r in refs], 0)


def softmax_tiles(keys, tiles, q_of, old_of, give):
    keys_t = keys.T

    def scores(tile):
        return dot(keys, q_of(*tile), ((1,), (0,)))

    following = scores(tiles[0])
    for i, tile in enumerate(tiles):
        s = following
        if i + 1 < len(tiles):
            following = scores(tiles[i + 1])
        old = old_of(*tile)
        m = jnp.max(s, 0, keepdims=True)
        if old is not None:
            m = jnp.maximum(m, old[0])
        p = jnp.exp2(s - m)
        total = jnp.sum(p, 0, keepdims=True)
        acc = dot(keys_t, p.astype(BF16), ((1,), (0,)))
        if old is not None:
            alpha = jnp.exp2(old[0] - m)
            total = total + alpha * old[1]
            acc = acc + alpha * old[2]
        give(*tile, (m, total, acc))


def tiles_of(low, high, size=512):
    return [(at, min(at + size, high)) for at in range(low, high, size)]


def attention_kernel(n_keys, n_q, n_state, n_out, low, high, *refs):
    keys = joined(refs[:n_keys])
    queries = refs[n_keys : n_keys + n_q]
    state = refs[n_keys + n_q : n_keys + n_q + 3 * n_state]
    outs = refs[n_keys + n_q + 3 * n_state :]

    def old_of(a, b):
        return [read(state[i::3], a, b) for i in range(3)] if n_state else None

    def give(a, b, values):
        for i, value in enumerate(values):
            write(outs[i::3], a - low, b - low, value)

    softmax_tiles(keys, tiles_of(low, high), lambda a, b: read(queries, a, b), old_of, give)


def attention_step(keys, queries, state=(), low=0, high=None):
    widths = [q.shape[1] for q in queries]
    high = sum(widths) if high is None else high
    rows = sum(k.shape[0] for k in keys)
    whole_state = bool(state) and high - low == sum(s[0].shape[1] for s in state)
    outs = [s[0].shape[1] for s in state] if whole_state else [high - low]
    flat = [v for s in state for v in s]
    before = len(keys) + len(queries)
    result = call(
        functools.partial(
            attention_kernel, len(keys), len(queries), len(state), len(outs), low, high
        ),
        [shape for n in outs for shape in (((1, n), F32), ((1, n), F32), ((C, n), F32))],
        *keys,
        *queries,
        *flat,
        name="attention_step",
        flops=4 * rows * (high - low) * C,
        nbytes=6e6,
        aliases={before + i: i for i in range(len(flat))} if whole_state else None,
    )
    return [tuple(result[i : i + 3]) for i in range(0, len(result), 3)]


def gate_kernel(*refs):
    pass


def after(values, *done):
    count = len(values)
    return call(
        gate_kernel,
        [(v.shape, v.dtype) for v in values],
        *values,
        *done,
        name="gate",
        flops=1,
        nbytes=1,
        specs=[ANY] * (count + len(done)),
        out_spec=ANY,
        aliases={i: i for i in range(count)},
    )


def split3(x):
    hi = x.astype(BF16)
    rest = x - hi.astype(F32)
    mid = rest.astype(BF16)
    low = (rest - mid.astype(F32)).astype(BF16)
    return hi, mid, low


def stat_rows(parts):
    n = parts[0].shape[1]
    row = lax.broadcasted_iota(jnp.int32, (STAT, n), 0)
    block = jnp.zeros((STAT, n), F32)
    for i, part in enumerate(parts):
        for j, piece in enumerate(split3(part)):
            block = jnp.where(row == 3 * i + j, piece.astype(F32), block)
    return block.astype(BF16)


def stat_of(block, i):
    b = block.astype(F32)
    return b[3 * i : 3 * i + 1] + b[3 * i + 1 : 3 * i + 2] + b[3 * i + 2 : 3 * i + 3]


def opposite_kernel(n_keys, *refs):
    q, m_old, l_old, acc_old, top, bottom = refs[n_keys:]

    def give(_a, _b, values):
        m, total, acc = values
        out = (acc / total).astype(BF16)
        stats = stat_rows([m + jnp.log2(total)])
        top[:HALF] = out[:HALF]
        top[HALF:] = stats
        bottom[:HALF] = out[HALF:]
        bottom[HALF:] = stats

    old = lambda a, b: (m_old[...], l_old[...], acc_old[...])
    softmax_tiles(joined(refs[:n_keys]), [(0, CELLS)], lambda a, b: q[...], old, give)


def opposite(keys, q_far, state):
    rows = sum(k.shape[0] for k in keys)
    return call(
        functools.partial(opposite_kernel, len(keys)),
        [((HALF + STAT, CELLS), BF16)] * 2,
        *keys,
        q_far,
        *state,
        name="opposite",
        flops=4 * rows * CELLS * C,
        nbytes=2e6,
    )


def merge(parts):
    top = functools.reduce(jnp.maximum, [s for s, _ in parts])
    w = [jnp.exp2(s - top) for s, _ in parts]
    total = functools.reduce(jnp.add, w)
    inverse = 1.0 / total
    out = functools.reduce(jnp.add, [(a * inverse) * o for a, (_, o) in zip(w, parts)])
    return top + jnp.log2(total), out


def relay_kernel(from_low, from_high, m, total, acc, _phases, to_low, to_high):
    for side, got, out in ((0, from_high, to_low), (1, from_low, to_high)):
        cols = slice(side * CELLS, (side + 1) * CELLS)
        stat = m[:, cols] + jnp.log2(total[:, cols])
        mine = acc[:, cols] / total[:, cols]
        theirs = (stat_of(got[HALF:], 0), got[:HALF].astype(F32))
        if side == 0:
            stat_t, half_t = stat, mine[:HALF]
            stat_b, half_b = merge([(stat, mine[HALF:]), theirs])
        else:
            stat_t, half_t = merge([(stat, mine[:HALF]), theirs])
            stat_b, half_b = stat, mine[HALF:]
        out[:HALF] = half_t.astype(BF16)
        out[HALF:C] = half_b.astype(BF16)
        out[C:] = stat_rows([stat_t, stat_b])


def finish_kernel(from_low, from_high, m, total, acc, shift, weight, wp, small, block, out):
    c = shift[...]
    stat = m[...] + jnp.log2(total[...]) + c
    mine = acc[...] / total[...]
    halves = []
    for i in range(2):
        rows = slice(i * HALF, (i + 1) * HALF)
        parts = [(stat, mine[rows])] + [
            (stat_of(got[C:], i) + c, got[rows].astype(F32)) for got in (from_low, from_high)
        ]
        halves.append(merge(parts)[1])
    mixed_in = jnp.concatenate(halves, 0).astype(BF16)
    mixed = (dot(mixed_in, weight[:, 2 * C :], ((0,), (0,))) + small[4:5, 2 * C :]).astype(BF16)
    attended = dot(mixed, wp[...], ((1,), (0,))) + small[3:4, :C] + block[...].astype(F32)
    out[...] = attended.astype(BF16)


def pack_kernel(flat, small):
    small[...] = jnp.zeros_like(small)
    at = 0
    for i, n in enumerate((C, C, C, C, 3 * C, OUT)):
        small[i, :n] = flat[at : at + n]
        at += n


def up_phases_kernel(weight, out):
    w = [[weight[b, c].astype(F32) for c in range(3)] for b in range(3)]

    def pairs(a, b, c):
        return ((a, b + c), (a + b, c))

    by_row = [pairs(*(w[b][c] for b in range(3))) for c in range(3)]
    for di in range(2):
        for rt in range(2):
            by_column = pairs(*(by_row[c][di][rt] for c in range(3)))
            for dj in range(2):
                for ct in range(2):
                    value = jnp.concatenate(
                        [by_column[dj][ct], jnp.zeros((256 - OUT, C), F32)], 0
                    )
                    out[di, dj, rt, ct * C : (ct + 1) * C] = value.T.astype(BF16)


def fill_plain(scratch, index, row):
    def store(variant, value):
        scratch[index, :, variant * C : (variant + 1) * C] = value

    col_variants(row.astype(F32), store)


def store_phase(wide, row, dj, value):
    for part in range(2):
        wide[part, row, pl.ds(dj, W, stride=2), :] = value[:, part * 128 : (part + 1) * 128]


def read_row(wide, row):
    return jnp.concatenate([wide[0, row].T, wide[1, row].T[: OUT - 128]], 0)


def up_inner_kernel(body, weight, small, out, edge, scratch, wide):
    for i in range(ROWS):
        fill_plain(scratch, i, body[i])
    b = small[5:6, :256]
    for di in range(2):
        for dj in range(2):
            full = scratch[:, :, dj * C : (dj + 2) * C].reshape(CELLS, 2 * C)
            if di == 0:
                here = dot(full, weight[0, dj, 1], ((1,), (0,))) + b
                beside = dot(full[: 2 * W], weight[0, dj, 0], ((1,), (0,)))
                parts = [here[:W], here[W : 2 * W] + beside[:W], here[2 * W :] + beside[W:]]
            else:
                here = dot(full, weight[1, dj, 0], ((1,), (0,))) + b
                beside = dot(full[W:], weight[1, dj, 1], ((1,), (0,)))
                parts = [here[:W] + beside[:W], here[W : 2 * W] + beside[W:], here[2 * W :]]
            for i, part in enumerate(parts):
                store_phase(wide, 2 * i + di, dj, part)
    for row in range(1, 2 * ROWS - 1):
        out[row] = read_row(wide, row).astype(BF16)
    edge[0] = read_row(wide, 0)
    edge[1] = read_row(wide, 2 * ROWS - 1)


def up_edges_kernel(low, high, weight, edge, _start, out, scratch, wide, rows, sem):
    _, _, above, below = inside()
    for i, (ref, present) in enumerate(((low, above), (high, below))):
        row = ref[0]
        fill_plain(scratch, i, jnp.where(present, row, jnp.zeros_like(row)))
    copies = []
    for side in range(2):
        for dj in range(2):
            left = scratch[side, :, dj * C : (dj + 2) * C]
            store_phase(wide, side, dj, dot(left, weight[side, dj, side], ((1,), (0,))))
        rows[side] = (edge[side] + read_row(wide, side)).astype(BF16)
        row = out.at[side * (2 * ROWS - 1)]
        copies.append(pltpu.make_async_copy(rows.at[side], row, sem.at[side]))
        copies[side].start()
    for copy in copies:
        copy.wait()


def permute_z(value, by):
    pairs = [(x * ZN + z, x * ZN + (z + by) % ZN) for x in range(XN) for z in range(ZN)]
    return lax.ppermute(value, "rows", pairs)


def permute_x(value, by):
    pairs = [(x * ZN + z, (x + by) % XN * ZN + z) for x in range(XN) for z in range(ZN)]
    return lax.ppermute(value, "rows", pairs)


def to_bands(value, by):
    n = XN * ZN
    return lax.ppermute(value, "rows", [(i, (i + by) % n) for i in range(n)])


def on_device(
    latent,
    norm1_gain,
    conv1_weight,
    conv1_bias,
    attention_gain,
    qkv_weight,
    qkv_bias,
    proj_weight,
    proj_bias,
    up_weight,
    up_bias,
):
    own = latent[0]
    two = lax.ppermute(own, "tm", [(t, (t + 2) % TN) for t in range(TN)])
    flat = (norm1_gain, conv1_bias, attention_gain, proj_bias, qkv_bias, up_bias)
    ends = [sum(v.shape[0] for v in flat[: i + 1]) for i in range(len(flat))]
    joined_flat = functools.reduce(
        jnp.add,
        [jnp.pad(v, (end - v.shape[0], ends[-1] - end)) for v, end in zip(flat, ends)],
    )
    small = call(pack_kernel, [((8, 3 * C), F32)], joined_flat, name="pack")
    acc, w_own, w_pair = conv_own(own, small, conv1_weight)
    pairs = [(t, t ^ 1) for t in range(TN)]
    to_next, to_previous, pair = call(
        edge_payload_kernel,
        [((2, W, C), BF16)] * 2 + [((ROWS, W, C), BF16)],
        own,
        two,
        acc,
        name="edge_payload",
        specs=[VM, VM, ANY],
    )
    low, high = to_bands(to_next, 1), to_bands(to_previous, -1)
    one = lax.ppermute(pair, "tm", pairs)
    acc = conv_earlier(two, one, small, w_pair, acc)
    pair_edges = call(
        pair_edges_kernel,
        [((2, W, C), BF16)],
        low,
        high,
        acc,
        name="pair_edges",
        specs=[VM, VM, ANY],
    )
    one_edges = lax.ppermute(pair_edges, "tm", pairs)
    acc = call(
        conv_edges_kernel,
        [((CELLS, C), F32)],
        low,
        high,
        small,
        w_own,
        w_pair,
        acc,
        name="conv_edges",
        flops=2 * CELLS * 2 * C * C,
        scratch=[pltpu.VMEM((4, W, 3 * C), BF16)],
        aliases={5: 0},
    )
    block, normed = call(
        conv_last_kernel,
        [((CELLS, C), BF16)] * 2,
        one_edges,
        own,
        small,
        w_pair,
        acc,
        name="conv_last",
        flops=2 * CELLS * C * C,
        scratch=[pltpu.VMEM((2, W, 3 * C), BF16)],
    )

    up, down = permute_z(normed, 1), permute_z(normed, -1)
    query, shift = call(
        query_kernel,
        [((C, CELLS), BF16), ((1, CELLS), F32)],
        normed,
        qkv_weight,
        small,
        name="queries",
        flops=4 * CELLS * C * C,
    )
    q_low, q_high = permute_x(query, 1), permute_x(query, -1)
    q_far = permute_x(query, 2)
    up2, down2 = permute_z(up, 1), permute_z(down, -1)
    early = [normed, up, down]
    near = [q_low, q_high, query]
    (state,) = attention_step(early, near)
    up2, down2 = after((up2, down2), state[0])
    up3, down3 = permute_z(up2, 1), permute_z(down2, -1)
    (far,) = attention_step(early, [q_far])
    queries = near + [q_far]
    state, far = attention_step([up2, down2], queries, (state, far))
    up4, down4 = permute_z(up3[: CELLS // 2], 1), permute_z(down3[CELLS // 2 :], -1)
    state, far = attention_step([up3, down3], queries, (state, far))
    last = [up4, down4]
    pay_t, pay_b = opposite(last, q_far, far)
    half_low, half_high = permute_x(pay_t, 1), permute_x(pay_b, -1)
    (sides,) = attention_step(last, near, (state,), 0, 2 * CELLS)
    phases = call(
        up_phases_kernel,
        [((2, 2, 2, 2 * C, 256), BF16)],
        up_weight.transpose(0, 1, 3, 2),
        name="up_phases",
        flops=1e7,
        nbytes=4e6,
    )
    to_low, to_high = call(
        relay_kernel,
        [((C + STAT, CELLS), BF16)] * 2,
        half_low,
        half_high,
        *sides,
        phases,
        name="relay",
        specs=[VM] * 5 + [ANY],
    )
    from_low, from_high = permute_x(to_high, 1), permute_x(to_low, -1)
    (mine,) = attention_step(last, near, (state,), 2 * CELLS, 3 * CELLS)
    attended = call(
        finish_kernel,
        [((CELLS, C), BF16)],
        from_low,
        from_high,
        *mine,
        shift,
        qkv_weight,
        proj_weight,
        small,
        block,
        name="finish",
        flops=4 * CELLS * C * C,
    ).reshape(ROWS, W, C)
    edge_low, edge_high = to_bands(attended[2:], 1), to_bands(attended[:1], -1)
    inner, edge = call(
        up_inner_kernel,
        [((2 * ROWS, OUT, 2 * W), BF16), ((2, OUT, 2 * W), F32)],
        attended,
        phases,
        small,
        name="up_inner",
        flops=2 * CELLS * 14 * C * OUT,
        scratch=[
            pltpu.VMEM((ROWS, W, 3 * C), BF16),
            pltpu.VMEM((2, 2 * ROWS, 2 * W, 128), F32),
        ],
    )
    result = call(
        up_edges_kernel,
        [((2 * ROWS, OUT, 2 * W), BF16)],
        edge_low,
        edge_high,
        phases,
        edge,
        inner,
        name="up_edges",
        flops=2 * CELLS * 2 * C * OUT,
        scratch=[
            pltpu.VMEM((2, W, 3 * C), BF16),
            pltpu.VMEM((2, 2, 2 * W, 128), F32),
            pltpu.VMEM((2, OUT, 2 * W), BF16),
            pltpu.SemaphoreType.DMA((2,)),
        ],
        specs=[VM, VM, VM, VM, ANY],
        out_spec=ANY,
        aliases={4: 0},
    )
    return result.transpose(0, 2, 1)[None]


def solution(mesh):
    return jax.shard_map(
        on_device,
        mesh=mesh,
        in_specs=(P("tm", "rows", None, None), P(), P(), P(), P(), P(), P(), P(), P(), P(), P()),
        out_specs=P("tm", "rows", None, None),
        check_vma=False,
    )
```

profile of v0, /device:TPU:16, one launch (start us, length us, event | category | flops | bytes accessed | tf_op | source)
XLA Modules:
  0.0 87.8 jit_solution(16854960674542096276)
XLA Ops:
  0.0 1.3 %collective-permute-start = (bf16[3,128,384]{2,1,0:T(8,128)(2,1)}, bf16[3,128,384]{2,1,0:T(8,128)(2,1)S(1)}, u32[]{:S(2)}, u32[]{:S(2)}) collective-permute-start(bf16[3,128,384]{2,1,0:T(8,128)(2,1)} %bitcast.10), channel_id=1, source_target_pairs={{0,64},{32,96},{64,128},{96,160},{128,192},{160,224},{192,0},{224,... | collective-permute-start | bytes 884744 | tf_op jit(solution)/shard_map/ppermute | solution.py:567
  1.3 0.8 pad_add_fusion.flat
  2.1 1.0 %copy-done.1 = bf16[1,3,128,384]{3,2,1,0:T(8,128)(2,1)S(1)} copy-done((bf16[1,3,128,384]{3,2,1,0:T(8,128)(2,1)S(1)}, bf16[1,3,128,384]{3,2,1,0:T(8,128)(2,1)}, u32[]{:S(2)}) %copy-start.1) | copy-done | bytes 294936
  3.0 4.2 %conv_own.1 = (f32[384,384]{1,0:T(8,128)S(1)}, bf16[2,3,384,384]{3,2,1,0:T(8,128)(2,1)S(1)}, bf16[2,3,3,384,384]{4,3,2,1,0:T(8,128)(2,1)S(1)}) custom-call(bf16[3,128,384]{2,1,0:T(8,128)(2,1)S(1)} %bitcast.11, f32[8,1152]{1,0:T(8,128)S(1)} %pack.1.small, bf16[3,3,3,384,384]{4,3,2,1,0:T(8,128)(2,1)} %weight.3), custom_call_target="tpu_custom_call" | custom-call | flops 1019215872 | bytes 1000000 | tf_op jit(solution)/shard_map/conv_own/pallas_call | solution.py:44
  7.2 1.7 %collective-permute-done.two = bf16[3,128,384]{2,1,0:T(8,128)(2,1)S(1)} collective-permute-done((bf16[3,128,384]{2,1,0:T(8,128)(2,1)}, bf16[3,128,384]{2,1,0:T(8,128)(2,1)S(1)}, u32[]{:S(2)}, u32[]{:S(2)}) %collective-permute-start) | collective-permute-done | bytes 294944 | tf_op jit(solution)/shard_map/ppermute | solution.py:567
  9.0 0.1 collective-permute-start.3
  9.1 2.0 %collective-permute-start.1 = (bf16[2,128,384]{2,1,0:T(8,128)(2,1)S(1)}, bf16[2,128,384]{2,1,0:T(8,128)(2,1)S(1)}, u32[]{:S(2)}, u32[]{:S(2)}) collective-permute-start(bf16[2,128,384]{2,1,0:T(8,128)(2,1)S(1)} %get-tuple-element.48), channel_id=1, source_target_pairs={{0,1},{1,2},{2,3},{3,4},{4,5},{5,6},{6,7},{7,8},{8,9},{9,10},{10,1... | collective-permute-start | bytes 589832 | tf_op jit(solution)/shard_map/ppermute | solution.py:550
  11.1 6.2 %collective-permute-start.2 = (bf16[2,128,384]{2,1,0:T(8,128)(2,1)S(1)}, bf16[2,128,384]{2,1,0:T(8,128)(2,1)S(1)}, u32[]{:S(2)}, u32[]{:S(2)}) collective-permute-start(bf16[2,128,384]{2,1,0:T(8,128)(2,1)S(1)} %get-tuple-element.49), channel_id=1, source_target_pairs={{0,31},{1,0},{2,1},{3,2},{4,3},{5,4},{6,5},{7,6},{8,7},{9,8},{10,9... | collective-permute-start | bytes 589832 | tf_op jit(solution)/shard_map/ppermute | solution.py:550
  17.4 4.9 %conv_earlier.1._acc.start = f32[384,384]{1,0:T(8,128)S(1)} custom-call(bf16[3,128,384]{2,1,0:T(8,128)(2,1)S(1)} %collective-permute-done.two, bf16[3,128,384]{2,1,0:T(8,128)(2,1)S(1)} %collective-permute-done.3.one, f32[8,1152]{1,0:T(8,128)S(1)} %pack.1.small, ...), custom_call_target="tpu_custom_call", output_to_operand_aliasing={{}: (4, {})} | custom-call | flops 2038431744 | bytes 1000000 | tf_op jit(solution)/shard_map/conv_earlier/pallas_call | solution.py:44
  22.2 0.5 collective-permute-done.1.low
  22.8 0.1 collective-permute-start.4
  22.9 1.2 %conv_edges.1.start = f32[384,384]{1,0:T(8,128)S(1)} custom-call(bf16[2,128,384]{2,1,0:T(8,128)(2,1)S(1)} %collective-permute-done.1.low, bf16[2,128,384]{2,1,0:T(8,128)(2,1)S(1)} %collective-permute-done.2.high, f32[8,1152]{1,0:T(8,128)S(1)} %pack.1.small, bf16[2,3,384,384]{3,2,1,0:T(8,128)(2,1)S(1)} %get-tuple-element.52.w_own, ...), custom_call_target="tpu_custom_call", output_to_operand_aliasing={{}: (5, {})} | custom-call | flops 226492416 | bytes 1000000 | tf_op jit(solution)/shard_map/conv_edges/pallas_call | solution.py:44
  24.1 0.2 collective-permute-done.4.edges
  24.3 0.9 conv_last.1
  25.2 0.1 collective-permute-start.5
  25.2 3.2 %collective-permute-start.7 = (bf16[384,384]{1,0:T(8,128)(2,1)S(1)}, bf16[384,384]{1,0:T(8,128)(2,1)S(1)}, u32[]{:S(2)}, u32[]{:S(2)}) collective-permute-start(bf16[384,384]{1,0:T(8,128)(2,1)S(1)} %get-tuple-element.53.normed.refs_0_), channel_id=1, source_target_pairs={{0,7},{1,0},{2,1},{3,2},{4,3},{5,4},{6,5},{7,6},{8,15},{9,8},{10,9... | collective-permute-start | bytes 884744 | tf_op jit(solution)/shard_map/ppermute | solution.py:540
  28.5 0.7 queries.1
  29.2 3.2 %collective-permute-start.10 = (bf16[384,384]{1,0:T(8,128)(2,1)S(1)}, bf16[384,384]{1,0:T(8,128)(2,1)S(1)}, u32[]{:S(2)}, u32[]{:S(2)}) collective-permute-start(bf16[384,384]{1,0:T(8,128)(2,1)S(1)} %get-tuple-element.54.refs_5_.refs_4_), channel_id=1, source_target_pairs={{0,24},{1,25},{2,26},{3,27},{4,28},{5,29},{6,30},{7,31},{8,0},{9,1... | collective-permute-start | bytes 884744 | tf_op jit(solution)/shard_map/ppermute | solution.py:545
  32.5 3.2 %collective-permute-done.5.refs_1_ = bf16[384,384]{1,0:T(8,128)(2,1)S(1)} collective-permute-done((bf16[384,384]{1,0:T(8,128)(2,1)S(1)}, bf16[384,384]{1,0:T(8,128)(2,1)S(1)}, u32[]{:S(2)}, u32[]{:S(2)}) %collective-permute-start.5) | collective-permute-done | bytes 294944 | tf_op jit(solution)/shard_map/ppermute | solution.py:540
  35.7 3.2 %collective-permute-start.8 = (bf16[384,384]{1,0:T(8,128)(2,1)S(1)}, bf16[384,384]{1,0:T(8,128)(2,1)S(1)}, u32[]{:S(2)}, u32[]{:S(2)}) collective-permute-start(bf16[384,384]{1,0:T(8,128)(2,1)S(1)} %collective-permute-done.7.refs_2_), channel_id=1, source_target_pairs={{0,7},{1,0},{2,1},{3,2},{4,3},{5,4},{6,5},{7,6},{8,15},{9,8},{10,9... | collective-permute-start | bytes 884744 | tf_op jit(solution)/shard_map/ppermute | solution.py:540
  38.9 1.7 %collective-permute-start.15 = (bf16[384,384]{1,0:T(8,128)(2,1)S(1)}, bf16[384,384]{1,0:T(8,128)(2,1)S(1)}, u32[]{:S(2)}, u32[]{:S(2)}) collective-permute-start(bf16[384,384]{1,0:T(8,128)(2,1)S(1)} %get-tuple-element.54.refs_5_.refs_4_), channel_id=1, source_target_pairs={{0,16},{1,17},{2,18},{3,19},{4,20},{5,21},{6,22},{7,23},{8,24},{9,... | collective-permute-start | bytes 884744 | tf_op jit(solution)/shard_map/ppermute | solution.py:545
  40.6 3.2 %attention_step.6 = (f32[1,1152]{1,0:T(1,128)S(1)}, f32[1,1152]{1,0:T(1,128)S(1)}, f32[384,1152]{1,0:T(8,128)S(1)}) custom-call(bf16[384,384]{1,0:T(8,128)(2,1)S(1)} %get-tuple-element.53.normed.refs_0_, bf16[384,384]{1,0:T(8,128)(2,1)S(1)} %collective-permute-done.5.refs_1_, bf16[384,384]{1,0:T(8,128)(2,1)S(1)} %collective-permute-done.7.refs_2_, ...), custom_call_target="tpu_custom_call" | custom-call | flops 2038431744 | bytes 6000000 | tf_op jit(solution)/shard_map/attention_step/pallas_call | solution.py:44
  43.9 1.4 %collective-permute-done.6.refs_0_ = bf16[384,384]{1,0:T(8,128)(2,1)S(1)} collective-permute-done((bf16[384,384]{1,0:T(8,128)(2,1)S(1)}, bf16[384,384]{1,0:T(8,128)(2,1)S(1)}, u32[]{:S(2)}, u32[]{:S(2)}) %collective-permute-start.6) | collective-permute-done | bytes 294944 | tf_op jit(solution)/shard_map/ppermute | solution.py:540
  45.3 3.2 %collective-permute-start.13 = (bf16[384,384]{1,0:T(8,128)(2,1)S(1)}, bf16[384,384]{1,0:T(8,128)(2,1)S(1)}, u32[]{:S(2)}, u32[]{:S(2)}) collective-permute-start(bf16[384,384]{1,0:T(8,128)(2,1)S(1)} %get-tuple-element.57.refs_1_), channel_id=1, source_target_pairs={{0,7},{1,0},{2,1},{3,2},{4,3},{5,4},{6,5},{7,6},{8,15},{9,8},{10,9... | collective-permute-start | bytes 884744 | tf_op jit(solution)/shard_map/ppermute | solution.py:540
  48.5 1.6 %attention_step.7 = (f32[1,384]{1,0:T(1,128)S(1)}, f32[1,384]{1,0:T(1,128)S(1)}, f32[384,384]{1,0:T(8,128)S(1)}) custom-call(bf16[384,384]{1,0:T(8,128)(2,1)S(1)} %get-tuple-element.53.normed.refs_0_, bf16[384,384]{1,0:T(8,128)(2,1)S(1)} %collective-permute-done.5.refs_1_, bf16[384,384]{1,0:T(8,128)(2,1)S(1)} %collective-permute-done.7.refs_2_, ...), custom_call_target="tpu_custom_call" | custom-call | flops 679477248 | bytes 6000000 | tf_op jit(solution)/shard_map/attention_step/pallas_call | solution.py:44
  50.1 3.2 %attention_step.8 = (f32[1,1152]{1,0:T(1,128)S(1)}, f32[1,1152]{1,0:T(1,128)S(1)}, f32[384,1152]{1,0:T(8,128)S(1)}, f32[1,384]{1,0:T(1,128)S(1)}, f32[1,384]{1,0:T(1,128)S(1)}, /*index=5*/f32[384,384]{1,0:T(8,128)S(1)}) custom-call(bf16[384,384]{1,0:T(8,128)(2,1)S(1)} %get-tuple-element., ...), custom_call_target="tpu_custom_call", output_to_operand_aliasing={{0}: (6, {}), {1}: (7, {}), {2}: (8, {}), {3}: (9, {}), {4}... | custom-call | flops 1811939328 | bytes 6000000 | tf_op jit(solution)/shard_map/attention_step/pallas_call | solution.py:44
  53.3 0.7 collective-permute-done.11.refs_0_
  54.0 0.1 collective-permute-start.12
  54.1 3.5 %collective-permute-start.14 = (bf16[192,384]{1,0:T(8,128)(2,1)S(1)}, bf16[192,384]{1,0:T(8,128)(2,1)S(1)}, u32[]{:S(2)}, u32[]{:S(2)}) collective-permute-start(bf16[192,384]{1,0:T(8,128)(2,1)S(1)} %slice.25), channel_id=1, source_target_pairs={{0,7},{1,0},{2,1},{3,2},{4,3},{5,4},{6,5},{7,6},{8,15},{9,8},{10,9... | collective-permute-start | bytes 442376 | tf_op jit(solution)/shard_map/ppermute | solution.py:540
  57.6 3.1 %attention_step.9 = (f32[1,1152]{1,0:T(1,128)S(1)}, f32[1,1152]{1,0:T(1,128)S(1)}, f32[384,1152]{1,0:T(8,128)S(1)}, f32[1,384]{1,0:T(1,128)S(1)}, f32[1,384]{1,0:T(1,128)S(1)}, /*index=5*/f32[384,384]{1,0:T(8,128)S(1)}) custom-call(bf16[384,384]{1,0:T(8,128)(2,1)S(1)} %collective-permute, ...), custom_call_target="tpu_custom_call", output_to_operand_aliasing={{0}: (6, {}), {1}: (7, {}), {2}: (8, {}), {3}: (9, {}), {4}... | custom-call | flops 1811939328 | bytes 6000000 | tf_op jit(solution)/shard_map/attention_step/pallas_call | solution.py:44
  60.8 0.8 opposite.1
  61.6 1.0 %collective-permute-start.16 = (bf16[208,384]{1,0:T(8,128)(2,1)S(1)}, bf16[208,384]{1,0:T(8,128)(2,1)S(1)}, u32[]{:S(2)}, u32[]{:S(2)}) collective-permute-start(bf16[208,384]{1,0:T(8,128)(2,1)S(1)} %get-tuple-element.72), channel_id=1, source_target_pairs={{0,8},{1,9},{2,10},{3,11},{4,12},{5,13},{6,14},{7,15},{8,16},{9,17... | collective-permute-start | bytes 479240 | tf_op jit(solution)/shard_map/ppermute | solution.py:545
  62.6 2.6 %collective-permute-start.17 = (bf16[208,384]{1,0:T(8,128)(2,1)S(1)}, bf16[208,384]{1,0:T(8,128)(2,1)S(1)}, u32[]{:S(2)}, u32[]{:S(2)}) collective-permute-start(bf16[208,384]{1,0:T(8,128)(2,1)S(1)} %get-tuple-element.73), channel_id=1, source_target_pairs={{0,24},{1,25},{2,26},{3,27},{4,28},{5,29},{6,30},{7,31},{8,0},{9,1... | collective-permute-start | bytes 479240 | tf_op jit(solution)/shard_map/ppermute | solution.py:545
  65.2 1.0 %up_phases.1._phases.weight = bf16[2,2,2,768,256]{4,3,2,1,0:T(8,128)(2,1)S(1)} custom-call(bf16[3,3,192,384]{3,2,1,0:T(8,128)(2,1)S(1)} %bitcast.15), custom_call_target="tpu_custom_call" | custom-call | flops 10000000 | bytes 4000000 | tf_op jit(solution)/shard_map/up_phases/pallas_call | solution.py:44
  66.1 1.0 %attention_step.10 = (f32[1,768]{1,0:T(1,128)S(1)}, f32[1,768]{1,0:T(1,128)S(1)}, f32[384,768]{1,0:T(8,128)S(1)}) custom-call(bf16[192,384]{1,0:T(8,128)(2,1)S(1)} %collective-permute-done.12.refs_0_, bf16[192,384]{1,0:T(8,128)(2,1)S(1)} %collective-permute-done.14.refs_1_, bf16[384,384]{1,0:T(8,128)(2,1)S(1)} %collective-permute-done.9.refs_3_.refs_2_, ...), custom_call_target="tpu_custom_call" | custom-call | flops 452984832 | bytes 6000000 | tf_op jit(solution)/shard_map/attention_step/pallas_call | solution.py:44
  67.2 1.1 %collective-permute-done.16.from_low = bf16[208,384]{1,0:T(8,128)(2,1)S(1)} collective-permute-done((bf16[208,384]{1,0:T(8,128)(2,1)S(1)}, bf16[208,384]{1,0:T(8,128)(2,1)S(1)}, u32[]{:S(2)}, u32[]{:S(2)}) %collective-permute-start.16) | collective-permute-done | bytes 159776 | tf_op jit(solution)/shard_map/ppermute | solution.py:545
  68.3 0.2 relay.1
  68.6 1.5 %collective-permute-start.18 = (bf16[400,384]{1,0:T(8,128)(2,1)S(1)}, bf16[400,384]{1,0:T(8,128)(2,1)S(1)}, u32[]{:S(2)}, u32[]{:S(2)}) collective-permute-start(bf16[400,384]{1,0:T(8,128)(2,1)S(1)} %get-tuple-element.80), channel_id=1, source_target_pairs={{0,8},{1,9},{2,10},{3,11},{4,12},{5,13},{6,14},{7,15},{8,16},{9,17... | collective-permute-start | bytes 921608 | tf_op jit(solution)/shard_map/ppermute | solution.py:545
  70.1 2.0 %collective-permute-start.19 = (bf16[400,384]{1,0:T(8,128)(2,1)S(1)}, bf16[400,384]{1,0:T(8,128)(2,1)S(1)}, u32[]{:S(2)}, u32[]{:S(2)}) collective-permute-start(bf16[400,384]{1,0:T(8,128)(2,1)S(1)} %get-tuple-element.81), channel_id=1, source_target_pairs={{0,24},{1,25},{2,26},{3,27},{4,28},{5,29},{6,30},{7,31},{8,0},{9,1... | collective-permute-start | bytes 921608 | tf_op jit(solution)/shard_map/ppermute | solution.py:545
  72.0 0.8 attention_step.11
  72.8 3.9 %collective-permute-done.18.from_low = bf16[400,384]{1,0:T(8,128)(2,1)S(1)} collective-permute-done((bf16[400,384]{1,0:T(8,128)(2,1)S(1)}, bf16[400,384]{1,0:T(8,128)(2,1)S(1)}, u32[]{:S(2)}, u32[]{:S(2)}) %collective-permute-start.18) | collective-permute-done | bytes 307232 | tf_op jit(solution)/shard_map/ppermute | solution.py:545
  76.8 0.1 collective-permute-done.19.from_high
  76.9 0.8 finish.1
  77.7 0.1 collective-permute-start.20
  77.8 6.2 %collective-permute-start.21 = (bf16[1,128,384]{2,1,0:T(8,128)(2,1)S(1)}, bf16[1,128,384]{2,1,0:T(8,128)(2,1)S(1)}, u32[]{:S(2)}, u32[]{:S(2)}) collective-permute-start(bf16[1,128,384]{2,1,0:T(8,128)(2,1)S(1)} %get-tuple-element.89), channel_id=1, source_target_pairs={{0,31},{1,0},{2,1},{3,2},{4,3},{5,4},{6,5},{7,6},{8,7},{9,8},{10,9... | collective-permute-start | bytes 294920 | tf_op jit(solution)/shard_map/ppermute | solution.py:550
  84.0 2.2 %up_inner.1 = (bf16[6,192,256]{2,1,0:T(8,128)(2,1)}, f32[2,192,256]{2,1,0:T(8,128)S(1)}) custom-call(bf16[3,128,384]{2,1,0:T(8,128)(2,1)S(1)} %bitcast.14, bf16[2,2,2,768,256]{4,3,2,1,0:T(8,128)(2,1)S(1)} %up_phases.1._phases.weight, f32[8,1152]{1,0:T(8,128)S(1)} %pack.1.small), custom_call_target="tpu_custom_call" | custom-call | flops 792723456 | bytes 1000000 | tf_op jit(solution)/shard_map/up_inner/pallas_call | solution.py:44
  86.2 0.3 collective-permute-done.20.low
  86.5 1.2 %up_edges.1 = bf16[6,192,256]{2,1,0:T(8,128)(2,1)} custom-call(bf16[1,128,384]{2,1,0:T(8,128)(2,1)S(1)} %collective-permute-done.20.low, bf16[1,128,384]{2,1,0:T(8,128)(2,1)S(1)} %collective-permute-done.21.high, bf16[2,2,2,768,256]{4,3,2,1,0:T(8,128)(2,1)S(1)} %up_phases.1._phases.weight, ...), custom_call_target="tpu_custom_call", output_to_operand_aliasing={{}: (4, {})} | custom-call | flops 113246208 | bytes 1000000 | tf_op jit(solution)/shard_map/up_edges/pallas_call | solution.py:44
  (29 shorter events, 0.3 us)
Async XLA Ops:
  0.0 9.0 %collective-permute-start = (bf16[3,128,384]{2,1,0:T(8,128)(2,1)}, bf16[3,128,384]{2,1,0:T(8,128)(2,1)S(1)}, u32[]{:S(2)}, u32[]{:S(2)}) collective-permute-start(bf16[3,128,384]{2,1,0:T(8,128)(2,1)} %bitcast.10), channel_id=1, source_target_pairs={{0,64},{32,96},{64,128},{96,160},{128,192},{160,224},{192,0},{224,... | collective-permute-start | bytes 884744 | tf_op jit(solution)/shard_map/ppermute | solution.py:567
  2.1 1.0 %copy-start.1 = (bf16[1,3,128,384]{3,2,1,0:T(8,128)(2,1)S(1)}, bf16[1,3,128,384]{3,2,1,0:T(8,128)(2,1)}, u32[]{:S(2)}) copy-start(bf16[1,3,128,384]{3,2,1,0:T(8,128)(2,1)} %param.11) | copy-start | bytes 884740
  9.0 8.3 %collective-permute-start.3 = (bf16[3,128,384]{2,1,0:T(8,128)(2,1)S(1)}, bf16[3,128,384]{2,1,0:T(8,128)(2,1)S(1)}, u32[]{:S(2)}, u32[]{:S(2)}) collective-permute-start(bf16[3,128,384]{2,1,0:T(8,128)(2,1)S(1)} %get-tuple-element.50), channel_id=1, source_target_pairs={{0,32},{32,0},{64,96},{96,64},{128,160},{160,128},{192,224},{224,1... | collective-permute-start | bytes 884744 | tf_op jit(solution)/shard_map/ppermute | solution.py:587
  9.1 13.6 %collective-permute-start.1 = (bf16[2,128,384]{2,1,0:T(8,128)(2,1)S(1)}, bf16[2,128,384]{2,1,0:T(8,128)(2,1)S(1)}, u32[]{:S(2)}, u32[]{:S(2)}) collective-permute-start(bf16[2,128,384]{2,1,0:T(8,128)(2,1)S(1)} %get-tuple-element.48), channel_id=1, source_target_pairs={{0,1},{1,2},{2,3},{3,4},{4,5},{5,6},{6,7},{7,8},{8,9},{9,10},{10,1... | collective-permute-start | bytes 589832 | tf_op jit(solution)/shard_map/ppermute | solution.py:550
  11.1 11.6 %collective-permute-start.2 = (bf16[2,128,384]{2,1,0:T(8,128)(2,1)S(1)}, bf16[2,128,384]{2,1,0:T(8,128)(2,1)S(1)}, u32[]{:S(2)}, u32[]{:S(2)}) collective-permute-start(bf16[2,128,384]{2,1,0:T(8,128)(2,1)S(1)} %get-tuple-element.49), channel_id=1, source_target_pairs={{0,31},{1,0},{2,1},{3,2},{4,3},{5,4},{6,5},{7,6},{8,7},{9,8},{10,9... | collective-permute-start | bytes 589832 | tf_op jit(solution)/shard_map/ppermute | solution.py:550
  22.8 1.5 %collective-permute-start.4 = (bf16[2,128,384]{2,1,0:T(8,128)(2,1)S(1)}, bf16[2,128,384]{2,1,0:T(8,128)(2,1)S(1)}, u32[]{:S(2)}, u32[]{:S(2)}) collective-permute-start(bf16[2,128,384]{2,1,0:T(8,128)(2,1)S(1)} %pair_edges.1), channel_id=1, source_target_pairs={{0,32},{32,0},{64,96},{96,64},{128,160},{160,128},{192,224},{224,1... | collective-permute-start | bytes 589832 | tf_op jit(solution)/shard_map/ppermute | solution.py:598
  24.1 4.4 %copy-start = (bf16[384,1152]{1,0:T(8,128)(2,1)S(1)}, bf16[384,1152]{1,0:T(8,128)(2,1)}, u32[]{:S(2)}) copy-start(bf16[384,1152]{1,0:T(8,128)(2,1)} %weight.5) | copy-start | bytes 2654212
  25.2 10.5 %collective-permute-start.5 = (bf16[384,384]{1,0:T(8,128)(2,1)S(1)}, bf16[384,384]{1,0:T(8,128)(2,1)S(1)}, u32[]{:S(2)}, u32[]{:S(2)}) collective-permute-start(bf16[384,384]{1,0:T(8,128)(2,1)S(1)} %get-tuple-element.53.normed.refs_0_), channel_id=1, source_target_pairs={{0,1},{1,2},{2,3},{3,4},{4,5},{5,6},{6,7},{7,0},{8,9},{9,10},{10,1... | collective-permute-start | bytes 884744 | tf_op jit(solution)/shard_map/ppermute | solution.py:540
  25.2 10.4 %collective-permute-start.7 = (bf16[384,384]{1,0:T(8,128)(2,1)S(1)}, bf16[384,384]{1,0:T(8,128)(2,1)S(1)}, u32[]{:S(2)}, u32[]{:S(2)}) collective-permute-start(bf16[384,384]{1,0:T(8,128)(2,1)S(1)} %get-tuple-element.53.normed.refs_0_), channel_id=1, source_target_pairs={{0,7},{1,0},{2,1},{3,2},{4,3},{5,4},{6,5},{7,6},{8,15},{9,8},{10,9... | collective-permute-start | bytes 884744 | tf_op jit(solution)/shard_map/ppermute | solution.py:540
  29.2 11.5 %collective-permute-start.9 = (bf16[384,384]{1,0:T(8,128)(2,1)S(1)}, bf16[384,384]{1,0:T(8,128)(2,1)S(1)}, u32[]{:S(2)}, u32[]{:S(2)}) collective-permute-start(bf16[384,384]{1,0:T(8,128)(2,1)S(1)} %get-tuple-element.54.refs_5_.refs_4_), channel_id=1, source_target_pairs={{0,8},{1,9},{2,10},{3,11},{4,12},{5,13},{6,14},{7,15},{8,16},{9,17... | collective-permute-start | bytes 884744 | tf_op jit(solution)/shard_map/ppermute | solution.py:545
  29.2 11.4 %collective-permute-start.10 = (bf16[384,384]{1,0:T(8,128)(2,1)S(1)}, bf16[384,384]{1,0:T(8,128)(2,1)S(1)}, u32[]{:S(2)}, u32[]{:S(2)}) collective-permute-start(bf16[384,384]{1,0:T(8,128)(2,1)S(1)} %get-tuple-element.54.refs_5_.refs_4_), channel_id=1, source_target_pairs={{0,24},{1,25},{2,26},{3,27},{4,28},{5,29},{6,30},{7,31},{8,0},{9,1... | collective-permute-start | bytes 884744 | tf_op jit(solution)/shard_map/ppermute | solution.py:545
  35.7 9.6 %collective-permute-start.6 = (bf16[384,384]{1,0:T(8,128)(2,1)S(1)}, bf16[384,384]{1,0:T(8,128)(2,1)S(1)}, u32[]{:S(2)}, u32[]{:S(2)}) collective-permute-start(bf16[384,384]{1,0:T(8,128)(2,1)S(1)} %collective-permute-done.5.refs_1_), channel_id=1, source_target_pairs={{0,1},{1,2},{2,3},{3,4},{4,5},{5,6},{6,7},{7,0},{8,9},{9,10},{10,1... | collective-permute-start | bytes 884744 | tf_op jit(solution)/shard_map/ppermute | solution.py:540
  35.7 9.6 %collective-permute-start.8 = (bf16[384,384]{1,0:T(8,128)(2,1)S(1)}, bf16[384,384]{1,0:T(8,128)(2,1)S(1)}, u32[]{:S(2)}, u32[]{:S(2)}) collective-permute-start(bf16[384,384]{1,0:T(8,128)(2,1)S(1)} %collective-permute-done.7.refs_2_), channel_id=1, source_target_pairs={{0,7},{1,0},{2,1},{3,2},{4,3},{5,4},{6,5},{7,6},{8,15},{9,8},{10,9... | collective-permute-start | bytes 884744 | tf_op jit(solution)/shard_map/ppermute | solution.py:540
  38.9 9.6 %collective-permute-start.15 = (bf16[384,384]{1,0:T(8,128)(2,1)S(1)}, bf16[384,384]{1,0:T(8,128)(2,1)S(1)}, u32[]{:S(2)}, u32[]{:S(2)}) collective-permute-start(bf16[384,384]{1,0:T(8,128)(2,1)S(1)} %get-tuple-element.54.refs_5_.refs_4_), channel_id=1, source_target_pairs={{0,16},{1,17},{2,18},{3,19},{4,20},{5,21},{6,22},{7,23},{8,24},{9,... | collective-permute-start | bytes 884744 | tf_op jit(solution)/shard_map/ppermute | solution.py:545
  45.3 8.7 %collective-permute-start.11 = (bf16[384,384]{1,0:T(8,128)(2,1)S(1)}, bf16[384,384]{1,0:T(8,128)(2,1)S(1)}, u32[]{:S(2)}, u32[]{:S(2)}) collective-permute-start(bf16[384,384]{1,0:T(8,128)(2,1)S(1)} %get-tuple-element.56.refs_0_), channel_id=1, source_target_pairs={{0,1},{1,2},{2,3},{3,4},{4,5},{5,6},{6,7},{7,0},{8,9},{9,10},{10,1... | collective-permute-start | bytes 884744 | tf_op jit(solution)/shard_map/ppermute | solution.py:540
  45.3 8.8 %collective-permute-start.13 = (bf16[384,384]{1,0:T(8,128)(2,1)S(1)}, bf16[384,384]{1,0:T(8,128)(2,1)S(1)}, u32[]{:S(2)}, u32[]{:S(2)}) collective-permute-start(bf16[384,384]{1,0:T(8,128)(2,1)S(1)} %get-tuple-element.57.refs_1_), channel_id=1, source_target_pairs={{0,7},{1,0},{2,1},{3,2},{4,3},{5,4},{6,5},{7,6},{8,15},{9,8},{10,9... | collective-permute-start | bytes 884744 | tf_op jit(solution)/shard_map/ppermute | solution.py:540
  54.0 6.8 %collective-permute-start.12 = (bf16[192,384]{1,0:T(8,128)(2,1)S(1)}, bf16[192,384]{1,0:T(8,128)(2,1)S(1)}, u32[]{:S(2)}, u32[]{:S(2)}) collective-permute-start(bf16[192,384]{1,0:T(8,128)(2,1)S(1)} %slice.24), channel_id=1, source_target_pairs={{0,1},{1,2},{2,3},{3,4},{4,5},{5,6},{6,7},{7,0},{8,9},{9,10},{10,1... | collective-permute-start | bytes 442376 | tf_op jit(solution)/shard_map/ppermute | solution.py:540
  54.1 6.7 %collective-permute-start.14 = (bf16[192,384]{1,0:T(8,128)(2,1)S(1)}, bf16[192,384]{1,0:T(8,128)(2,1)S(1)}, u32[]{:S(2)}, u32[]{:S(2)}) collective-permute-start(bf16[192,384]{1,0:T(8,128)(2,1)S(1)} %slice.25), channel_id=1, source_target_pairs={{0,7},{1,0},{2,1},{3,2},{4,3},{5,4},{6,5},{7,6},{8,15},{9,8},{10,9... | collective-permute-start | bytes 442376 | tf_op jit(solution)/shard_map/ppermute | solution.py:540
  57.6 7.5 %copy-start.2 = (bf16[3,3,384,192]{2,3,1,0:T(8,128)(2,1)S(1)}, bf16[3,3,384,192]{2,3,1,0:T(8,128)(2,1)}, u32[]{:S(2)}) copy-start(bf16[3,3,384,192]{2,3,1,0:T(8,128)(2,1)} %param.20) | copy-start | bytes 3981316
  61.6 6.7 %collective-permute-start.16 = (bf16[208,384]{1,0:T(8,128)(2,1)S(1)}, bf16[208,384]{1,0:T(8,128)(2,1)S(1)}, u32[]{:S(2)}, u32[]{:S(2)}) collective-permute-start(bf16[208,384]{1,0:T(8,128)(2,1)S(1)} %get-tuple-element.72), channel_id=1, source_target_pairs={{0,8},{1,9},{2,10},{3,11},{4,12},{5,13},{6,14},{7,15},{8,16},{9,17... | collective-permute-start | bytes 479240 | tf_op jit(solution)/shard_map/ppermute | solution.py:545
  62.6 5.7 %collective-permute-start.17 = (bf16[208,384]{1,0:T(8,128)(2,1)S(1)}, bf16[208,384]{1,0:T(8,128)(2,1)S(1)}, u32[]{:S(2)}, u32[]{:S(2)}) collective-permute-start(bf16[208,384]{1,0:T(8,128)(2,1)S(1)} %get-tuple-element.73), channel_id=1, source_target_pairs={{0,24},{1,25},{2,26},{3,27},{4,28},{5,29},{6,30},{7,31},{8,0},{9,1... | collective-permute-start | bytes 479240 | tf_op jit(solution)/shard_map/ppermute | solution.py:545
  68.6 8.4 %copy-start.3 = (bf16[384,384]{1,0:T(8,128)(2,1)S(1)}, bf16[384,384]{1,0:T(8,128)(2,1)}, u32[]{:S(2)}) copy-start(bf16[384,384]{1,0:T(8,128)(2,1)} %wp.1) | copy-start | bytes 884740
  68.6 8.2 %collective-permute-start.18 = (bf16[400,384]{1,0:T(8,128)(2,1)S(1)}, bf16[400,384]{1,0:T(8,128)(2,1)S(1)}, u32[]{:S(2)}, u32[]{:S(2)}) collective-permute-start(bf16[400,384]{1,0:T(8,128)(2,1)S(1)} %get-tuple-element.80), channel_id=1, source_target_pairs={{0,8},{1,9},{2,10},{3,11},{4,12},{5,13},{6,14},{7,15},{8,16},{9,17... | collective-permute-start | bytes 921608 | tf_op jit(solution)/shard_map/ppermute | solution.py:545
  70.1 6.9 %collective-permute-start.19 = (bf16[400,384]{1,0:T(8,128)(2,1)S(1)}, bf16[400,384]{1,0:T(8,128)(2,1)S(1)}, u32[]{:S(2)}, u32[]{:S(2)}) collective-permute-start(bf16[400,384]{1,0:T(8,128)(2,1)S(1)} %get-tuple-element.81), channel_id=1, source_target_pairs={{0,24},{1,25},{2,26},{3,27},{4,28},{5,29},{6,30},{7,31},{8,0},{9,1... | collective-permute-start | bytes 921608 | tf_op jit(solution)/shard_map/ppermute | solution.py:545
  77.7 8.8 %collective-permute-start.20 = (bf16[1,128,384]{2,1,0:T(8,128)(2,1)S(1)}, bf16[1,128,384]{2,1,0:T(8,128)(2,1)S(1)}, u32[]{:S(2)}, u32[]{:S(2)}) collective-permute-start(bf16[1,128,384]{2,1,0:T(8,128)(2,1)S(1)} %get-tuple-element.90), channel_id=1, source_target_pairs={{0,1},{1,2},{2,3},{3,4},{4,5},{5,6},{6,7},{7,8},{8,9},{9,10},{10,1... | collective-permute-start | bytes 294920 | tf_op jit(solution)/shard_map/ppermute | solution.py:550
  77.8 8.7 %collective-permute-start.21 = (bf16[1,128,384]{2,1,0:T(8,128)(2,1)S(1)}, bf16[1,128,384]{2,1,0:T(8,128)(2,1)S(1)}, u32[]{:S(2)}, u32[]{:S(2)}) collective-permute-start(bf16[1,128,384]{2,1,0:T(8,128)(2,1)S(1)} %get-tuple-element.89), channel_id=1, source_target_pairs={{0,31},{1,0},{2,1},{3,2},{4,3},{5,4},{6,5},{7,6},{8,7},{9,8},{10,9... | collective-permute-start | bytes 294920 | tf_op jit(solution)/shard_map/ppermute | solution.py:550
where the time goes:
time: 88 us; the launch traced here: 87.8 us
  starting transfers between devices  41.4 us (47%)
  Pallas kernels  31 us (35%)
  waiting for transfers between devices  13.3 us (15%)
  local copies, waits for them, and re-layouts  1.03 us (1%)
    pallas_call x21, Pallas kernels, call(): pl.pallas_call(body, in_specs=specs or [VM] * len(args), out_specs=[out_s...  31 us
    ppermute x4, starting transfers between devices, to_bands(): return lax.ppermute(value, 'rows', [(i, (i + by) % n) for i in range(n)])  14.5 us
    ppermute x8, starting transfers between devices, permute_z(): return lax.ppermute(value, 'rows', pairs)  13.4 us
    ppermute x7, starting transfers between devices, permute_x(): return lax.ppermute(value, 'rows', pairs)  12 us
    ppermute x8, waiting for transfers between devices, permute_z(): return lax.ppermute(value, 'rows', pairs)  5.31 us
    ppermute x7, waiting for transfers between devices, permute_x(): return lax.ppermute(value, 'rows', pairs)  5.2 us
  transfers between devices with their start and end apart: 22, of which 10 were waited for; matrix products, arithmetic and copies ran while one was open for 1% of the time, Pallas kernels for 31%

commit v1 on v0

--- a/solution.py
+++ b/solution.py
@@ -435,7 +435,7 @@
         out[C:] = stat_rows([stat_t, stat_b])
 
 
-def finish_kernel(from_low, from_high, m, total, acc, shift, weight, wp, small, block, out):
+def finish_kernel(from_low, from_high, m, total, acc, shift, weight, wp, small, block, out, to_next, to_previous):
     c = shift[...]
     stat = m[...] + jnp.log2(total[...]) + c
     mine = acc[...] / total[...]
@@ -449,7 +449,10 @@
     mixed_in = jnp.concatenate(halves, 0).astype(BF16)
     mixed = (dot(mixed_in, weight[:, 2 * C :], ((0,), (0,))) + small[4:5, 2 * C :]).astype(BF16)
     attended = dot(mixed, wp[...], ((1,), (0,))) + small[3:4, :C] + block[...].astype(F32)
-    out[...] = attended.astype(BF16)
+    attended = attended.astype(BF16)
+    out[...] = attended
+    to_next[0] = attended[2 * W :]
+    to_previous[0] = attended[:W]
 
 
 def pack_kernel(flat, small):
@@ -670,9 +673,9 @@
     )
     from_low, from_high = permute_x(to_high, 1), permute_x(to_low, -1)
     (mine,) = attention_step(last, near, (state,), 2 * CELLS, 3 * CELLS)
-    attended = call(
+    attended, to_next, to_previous = call(
         finish_kernel,
-        [((CELLS, C), BF16)],
+        [((CELLS, C), BF16)] + [((1, W, C), BF16)] * 2,
         from_low,
         from_high,
         *mine,
@@ -683,8 +686,9 @@
         block,
         name="finish",
         flops=4 * CELLS * C * C,
-    ).reshape(ROWS, W, C)
-    edge_low, edge_high = to_bands(attended[2:], 1), to_bands(attended[:1], -1)
+    )
+    attended = attended.reshape(ROWS, W, C)
+    edge_low, edge_high = to_bands(to_next, 1), to_bands(to_previous, -1)
     inner, edge = call(
         up_inner_kernel,
         [((2 * ROWS, OUT, 2 * W), BF16), ((2, OUT, 2 * W), F32)],

time: 88 us -> 88 us (level)
  no operation moved by 1% of the time
where the time goes in v1:
time: 88 us; the launch traced here: 87.8 us
  starting transfers between devices  41.4 us (47%)
  Pallas kernels  31 us (35%)
  waiting for transfers between devices  13.3 us (15%)
  local copies, waits for them, and re-layouts  1.01 us (1%)
    pallas_call x21, Pallas kernels, call(): pl.pallas_call(body, in_specs=specs or [VM] * len(args), out_specs=[out_s...  31 us
    ppermute x4, starting transfers between devices, to_bands(): return lax.ppermute(value, 'rows', [(i, (i + by) % n) for i in range(n)])  14.5 us
    ppermute x8, starting transfers between devices, permute_z(): return lax.ppermute(value, 'rows', pairs)  13.4 us
    ppermute x7, starting transfers between devices, permute_x(): return lax.ppermute(value, 'rows', pairs)  12 us
    ppermute x8, waiting for transfers between devices, permute_z(): return lax.ppermute(value, 'rows', pairs)  5.31 us
    ppermute x7, waiting for transfers between devices, permute_x(): return lax.ppermute(value, 'rows', pairs)  5.2 us
  transfers between devices with their start and end apart: 22, of which 10 were waited for; matrix products, arithmetic and copies ran while one was open for 1% of the time, Pallas kernels for 31%

profile of v1, /device:TPU:16, one launch (start us, length us, event | category | flops | bytes accessed | tf_op | source)
XLA Modules:
  0.0 87.8 jit_solution(13942584985093985629)
XLA Ops:
  0.0 1.3 %collective-permute-start = (bf16[3,128,384]{2,1,0:T(8,128)(2,1)}, bf16[3,128,384]{2,1,0:T(8,128)(2,1)S(1)}, u32[]{:S(2)}, u32[]{:S(2)}) collective-permute-start(bf16[3,128,384]{2,1,0:T(8,128)(2,1)} %bitcast.6), channel_id=1, source_target_pairs={{0,64},{32,96},{64,128},{96,160},{128,192},{160,224},{192,0},{224,... | collective-permute-start | bytes 884744 | tf_op jit(solution)/shard_map/ppermute | solution.py:570
  1.3 0.8 pad_add_fusion.flat
  2.1 1.0 %copy-done.1 = bf16[1,3,128,384]{3,2,1,0:T(8,128)(2,1)S(1)} copy-done((bf16[1,3,128,384]{3,2,1,0:T(8,128)(2,1)S(1)}, bf16[1,3,128,384]{3,2,1,0:T(8,128)(2,1)}, u32[]{:S(2)}) %copy-start.1) | copy-done | bytes 294936
  3.0 4.2 %conv_own.1 = (f32[384,384]{1,0:T(8,128)S(1)}, bf16[2,3,384,384]{3,2,1,0:T(8,128)(2,1)S(1)}, bf16[2,3,3,384,384]{4,3,2,1,0:T(8,128)(2,1)S(1)}) custom-call(bf16[3,128,384]{2,1,0:T(8,128)(2,1)S(1)} %bitcast.7, f32[8,1152]{1,0:T(8,128)S(1)} %pack.1.small, bf16[3,3,3,384,384]{4,3,2,1,0:T(8,128)(2,1)} %weight.3), custom_call_target="tpu_custom_call" | custom-call | flops 1019215872 | bytes 1000000 | tf_op jit(solution)/shard_map/conv_own/pallas_call | solution.py:44
  7.2 1.7 %collective-permute-done.two = bf16[3,128,384]{2,1,0:T(8,128)(2,1)S(1)} collective-permute-done((bf16[3,128,384]{2,1,0:T(8,128)(2,1)}, bf16[3,128,384]{2,1,0:T(8,128)(2,1)S(1)}, u32[]{:S(2)}, u32[]{:S(2)}) %collective-permute-start) | collective-permute-done | bytes 294944 | tf_op jit(solution)/shard_map/ppermute | solution.py:570
  9.0 0.1 collective-permute-start.3
  9.1 2.0 %collective-permute-start.1 = (bf16[2,128,384]{2,1,0:T(8,128)(2,1)S(1)}, bf16[2,128,384]{2,1,0:T(8,128)(2,1)S(1)}, u32[]{:S(2)}, u32[]{:S(2)}) collective-permute-start(bf16[2,128,384]{2,1,0:T(8,128)(2,1)S(1)} %get-tuple-element.51), channel_id=1, source_target_pairs={{0,1},{1,2},{2,3},{3,4},{4,5},{5,6},{6,7},{7,8},{8,9},{9,10},{10,1... | collective-permute-start | bytes 589832 | tf_op jit(solution)/shard_map/ppermute | solution.py:553
  11.1 6.2 %collective-permute-start.2 = (bf16[2,128,384]{2,1,0:T(8,128)(2,1)S(1)}, bf16[2,128,384]{2,1,0:T(8,128)(2,1)S(1)}, u32[]{:S(2)}, u32[]{:S(2)}) collective-permute-start(bf16[2,128,384]{2,1,0:T(8,128)(2,1)S(1)} %get-tuple-element.52), channel_id=1, source_target_pairs={{0,31},{1,0},{2,1},{3,2},{4,3},{5,4},{6,5},{7,6},{8,7},{9,8},{10,9... | collective-permute-start | bytes 589832 | tf_op jit(solution)/shard_map/ppermute | solution.py:553
  17.4 4.9 %conv_earlier.1._acc.start = f32[384,384]{1,0:T(8,128)S(1)} custom-call(bf16[3,128,384]{2,1,0:T(8,128)(2,1)S(1)} %collective-permute-done.two, bf16[3,128,384]{2,1,0:T(8,128)(2,1)S(1)} %collective-permute-done.3.one, f32[8,1152]{1,0:T(8,128)S(1)} %pack.1.small, ...), custom_call_target="tpu_custom_call", output_to_operand_aliasing={{}: (4, {})} | custom-call | flops 2038431744 | bytes 1000000 | tf_op jit(solution)/shard_map/conv_earlier/pallas_call | solution.py:44
  22.2 0.5 collective-permute-done.1.low
  22.8 0.1 collective-permute-start.4
  22.9 1.2 %conv_edges.1.start = f32[384,384]{1,0:T(8,128)S(1)} custom-call(bf16[2,128,384]{2,1,0:T(8,128)(2,1)S(1)} %collective-permute-done.1.low, bf16[2,128,384]{2,1,0:T(8,128)(2,1)S(1)} %collective-permute-done.2.high, f32[8,1152]{1,0:T(8,128)S(1)} %pack.1.small, bf16[2,3,384,384]{3,2,1,0:T(8,128)(2,1)S(1)} %get-tuple-element.55.w_own, ...), custom_call_target="tpu_custom_call", output_to_operand_aliasing={{}: (5, {})} | custom-call | flops 226492416 | bytes 1000000 | tf_op jit(solution)/shard_map/conv_edges/pallas_call | solution.py:44
  24.1 0.2 collective-permute-done.4.edges
  24.3 0.9 conv_last.1
  25.2 0.1 collective-permute-start.5
  25.2 3.2 %collective-permute-start.7 = (bf16[384,384]{1,0:T(8,128)(2,1)S(1)}, bf16[384,384]{1,0:T(8,128)(2,1)S(1)}, u32[]{:S(2)}, u32[]{:S(2)}) collective-permute-start(bf16[384,384]{1,0:T(8,128)(2,1)S(1)} %get-tuple-element.56.normed.refs_0_), channel_id=1, source_target_pairs={{0,7},{1,0},{2,1},{3,2},{4,3},{5,4},{6,5},{7,6},{8,15},{9,8},{10,9... | collective-permute-start | bytes 884744 | tf_op jit(solution)/shard_map/ppermute | solution.py:543
  28.5 0.7 queries.1
  29.2 3.2 %collective-permute-start.10 = (bf16[384,384]{1,0:T(8,128)(2,1)S(1)}, bf16[384,384]{1,0:T(8,128)(2,1)S(1)}, u32[]{:S(2)}, u32[]{:S(2)}) collective-permute-start(bf16[384,384]{1,0:T(8,128)(2,1)S(1)} %get-tuple-element.57.refs_5_.refs_4_), channel_id=1, source_target_pairs={{0,24},{1,25},{2,26},{3,27},{4,28},{5,29},{6,30},{7,31},{8,0},{9,1... | collective-permute-start | bytes 884744 | tf_op jit(solution)/shard_map/ppermute | solution.py:548
  32.5 3.2 %collective-permute-done.5.refs_1_ = bf16[384,384]{1,0:T(8,128)(2,1)S(1)} collective-permute-done((bf16[384,384]{1,0:T(8,128)(2,1)S(1)}, bf16[384,384]{1,0:T(8,128)(2,1)S(1)}, u32[]{:S(2)}, u32[]{:S(2)}) %collective-permute-start.5) | collective-permute-done | bytes 294944 | tf_op jit(solution)/shard_map/ppermute | solution.py:543
  35.7 3.2 %collective-permute-start.8 = (bf16[384,384]{1,0:T(8,128)(2,1)S(1)}, bf16[384,384]{1,0:T(8,128)(2,1)S(1)}, u32[]{:S(2)}, u32[]{:S(2)}) collective-permute-start(bf16[384,384]{1,0:T(8,128)(2,1)S(1)} %collective-permute-done.7.refs_2_), channel_id=1, source_target_pairs={{0,7},{1,0},{2,1},{3,2},{4,3},{5,4},{6,5},{7,6},{8,15},{9,8},{10,9... | collective-permute-start | bytes 884744 | tf_op jit(solution)/shard_map/ppermute | solution.py:543
  38.9 1.7 %collective-permute-start.15 = (bf16[384,384]{1,0:T(8,128)(2,1)S(1)}, bf16[384,384]{1,0:T(8,128)(2,1)S(1)}, u32[]{:S(2)}, u32[]{:S(2)}) collective-permute-start(bf16[384,384]{1,0:T(8,128)(2,1)S(1)} %get-tuple-element.57.refs_5_.refs_4_), channel_id=1, source_target_pairs={{0,16},{1,17},{2,18},{3,19},{4,20},{5,21},{6,22},{7,23},{8,24},{9,... | collective-permute-start | bytes 884744 | tf_op jit(solution)/shard_map/ppermute | solution.py:548
  40.6 3.2 %attention_step.6 = (f32[1,1152]{1,0:T(1,128)S(1)}, f32[1,1152]{1,0:T(1,128)S(1)}, f32[384,1152]{1,0:T(8,128)S(1)}) custom-call(bf16[384,384]{1,0:T(8,128)(2,1)S(1)} %get-tuple-element.56.normed.refs_0_, bf16[384,384]{1,0:T(8,128)(2,1)S(1)} %collective-permute-done.5.refs_1_, bf16[384,384]{1,0:T(8,128)(2,1)S(1)} %collective-permute-done.7.refs_2_, ...), custom_call_target="tpu_custom_call" | custom-call | flops 2038431744 | bytes 6000000 | tf_op jit(solution)/shard_map/attention_step/pallas_call | solution.py:44
  43.9 1.4 %collective-permute-done.6.refs_0_ = bf16[384,384]{1,0:T(8,128)(2,1)S(1)} collective-permute-done((bf16[384,384]{1,0:T(8,128)(2,1)S(1)}, bf16[384,384]{1,0:T(8,128)(2,1)S(1)}, u32[]{:S(2)}, u32[]{:S(2)}) %collective-permute-start.6) | collective-permute-done | bytes 294944 | tf_op jit(solution)/shard_map/ppermute | solution.py:543
  45.3 3.2 %collective-permute-start.13 = (bf16[384,384]{1,0:T(8,128)(2,1)S(1)}, bf16[384,384]{1,0:T(8,128)(2,1)S(1)}, u32[]{:S(2)}, u32[]{:S(2)}) collective-permute-start(bf16[384,384]{1,0:T(8,128)(2,1)S(1)} %get-tuple-element.60.refs_1_), channel_id=1, source_target_pairs={{0,7},{1,0},{2,1},{3,2},{4,3},{5,4},{6,5},{7,6},{8,15},{9,8},{10,9... | collective-permute-start | bytes 884744 | tf_op jit(solution)/shard_map/ppermute | solution.py:543
  48.5 1.6 %attention_step.7 = (f32[1,384]{1,0:T(1,128)S(1)}, f32[1,384]{1,0:T(1,128)S(1)}, f32[384,384]{1,0:T(8,128)S(1)}) custom-call(bf16[384,384]{1,0:T(8,128)(2,1)S(1)} %get-tuple-element.56.normed.refs_0_, bf16[384,384]{1,0:T(8,128)(2,1)S(1)} %collective-permute-done.5.refs_1_, bf16[384,384]{1,0:T(8,128)(2,1)S(1)} %collective-permute-done.7.refs_2_, ...), custom_call_target="tpu_custom_call" | custom-call | flops 679477248 | bytes 6000000 | tf_op jit(solution)/shard_map/attention_step/pallas_call | solution.py:44
  50.1 3.2 %attention_step.8 = (f32[1,1152]{1,0:T(1,128)S(1)}, f32[1,1152]{1,0:T(1,128)S(1)}, f32[384,1152]{1,0:T(8,128)S(1)}, f32[1,384]{1,0:T(1,128)S(1)}, f32[1,384]{1,0:T(1,128)S(1)}, /*index=5*/f32[384,384]{1,0:T(8,128)S(1)}) custom-call(bf16[384,384]{1,0:T(8,128)(2,1)S(1)} %get-tuple-element., ...), custom_call_target="tpu_custom_call", output_to_operand_aliasing={{0}: (6, {}), {1}: (7, {}), {2}: (8, {}), {3}: (9, {}), {4}... | custom-call | flops 1811939328 | bytes 6000000 | tf_op jit(solution)/shard_map/attention_step/pallas_call | solution.py:44
  53.3 0.7 collective-permute-done.11.refs_0_
  54.0 0.1 collective-permute-start.12
  54.1 3.5 %collective-permute-start.14 = (bf16[192,384]{1,0:T(8,128)(2,1)S(1)}, bf16[192,384]{1,0:T(8,128)(2,1)S(1)}, u32[]{:S(2)}, u32[]{:S(2)}) collective-permute-start(bf16[192,384]{1,0:T(8,128)(2,1)S(1)} %slice.9), channel_id=1, source_target_pairs={{0,7},{1,0},{2,1},{3,2},{4,3},{5,4},{6,5},{7,6},{8,15},{9,8},{10,9... | collective-permute-start | bytes 442376 | tf_op jit(solution)/shard_map/ppermute | solution.py:543
  57.6 3.1 %attention_step.9 = (f32[1,1152]{1,0:T(1,128)S(1)}, f32[1,1152]{1,0:T(1,128)S(1)}, f32[384,1152]{1,0:T(8,128)S(1)}, f32[1,384]{1,0:T(1,128)S(1)}, f32[1,384]{1,0:T(1,128)S(1)}, /*index=5*/f32[384,384]{1,0:T(8,128)S(1)}) custom-call(bf16[384,384]{1,0:T(8,128)(2,1)S(1)} %collective-permute, ...), custom_call_target="tpu_custom_call", output_to_operand_aliasing={{0}: (6, {}), {1}: (7, {}), {2}: (8, {}), {3}: (9, {}), {4}... | custom-call | flops 1811939328 | bytes 6000000 | tf_op jit(solution)/shard_map/attention_step/pallas_call | solution.py:44
  60.8 0.8 opposite.1
  61.6 1.0 %collective-permute-start.16 = (bf16[208,384]{1,0:T(8,128)(2,1)S(1)}, bf16[208,384]{1,0:T(8,128)(2,1)S(1)}, u32[]{:S(2)}, u32[]{:S(2)}) collective-permute-start(bf16[208,384]{1,0:T(8,128)(2,1)S(1)} %get-tuple-element.75), channel_id=1, source_target_pairs={{0,8},{1,9},{2,10},{3,11},{4,12},{5,13},{6,14},{7,15},{8,16},{9,17... | collective-permute-start | bytes 479240 | tf_op jit(solution)/shard_map/ppermute | solution.py:548
  62.6 2.6 %collective-permute-start.17 = (bf16[208,384]{1,0:T(8,128)(2,1)S(1)}, bf16[208,384]{1,0:T(8,128)(2,1)S(1)}, u32[]{:S(2)}, u32[]{:S(2)}) collective-permute-start(bf16[208,384]{1,0:T(8,128)(2,1)S(1)} %get-tuple-element.76), channel_id=1, source_target_pairs={{0,24},{1,25},{2,26},{3,27},{4,28},{5,29},{6,30},{7,31},{8,0},{9,1... | collective-permute-start | bytes 479240 | tf_op jit(solution)/shard_map/ppermute | solution.py:548
  65.2 1.0 %up_phases.1._phases.weight = bf16[2,2,2,768,256]{4,3,2,1,0:T(8,128)(2,1)S(1)} custom-call(bf16[3,3,192,384]{3,2,1,0:T(8,128)(2,1)S(1)} %bitcast.10), custom_call_target="tpu_custom_call" | custom-call | flops 10000000 | bytes 4000000 | tf_op jit(solution)/shard_map/up_phases/pallas_call | solution.py:44
  66.1 1.0 %attention_step.10 = (f32[1,768]{1,0:T(1,128)S(1)}, f32[1,768]{1,0:T(1,128)S(1)}, f32[384,768]{1,0:T(8,128)S(1)}) custom-call(bf16[192,384]{1,0:T(8,128)(2,1)S(1)} %collective-permute-done.12.refs_0_, bf16[192,384]{1,0:T(8,128)(2,1)S(1)} %collective-permute-done.14.refs_1_, bf16[384,384]{1,0:T(8,128)(2,1)S(1)} %collective-permute-done.9.refs_3_.refs_2_, ...), custom_call_target="tpu_custom_call" | custom-call | flops 452984832 | bytes 6000000 | tf_op jit(solution)/shard_map/attention_step/pallas_call | solution.py:44
  67.2 1.1 %collective-permute-done.16.from_low = bf16[208,384]{1,0:T(8,128)(2,1)S(1)} collective-permute-done((bf16[208,384]{1,0:T(8,128)(2,1)S(1)}, bf16[208,384]{1,0:T(8,128)(2,1)S(1)}, u32[]{:S(2)}, u32[]{:S(2)}) %collective-permute-start.16) | collective-permute-done | bytes 159776 | tf_op jit(solution)/shard_map/ppermute | solution.py:548
  68.3 0.2 relay.1
  68.6 1.5 %collective-permute-start.18 = (bf16[400,384]{1,0:T(8,128)(2,1)S(1)}, bf16[400,384]{1,0:T(8,128)(2,1)S(1)}, u32[]{:S(2)}, u32[]{:S(2)}) collective-permute-start(bf16[400,384]{1,0:T(8,128)(2,1)S(1)} %get-tuple-element.83), channel_id=1, source_target_pairs={{0,8},{1,9},{2,10},{3,11},{4,12},{5,13},{6,14},{7,15},{8,16},{9,17... | collective-permute-start | bytes 921608 | tf_op jit(solution)/shard_map/ppermute | solution.py:548
  70.1 2.0 %collective-permute-start.19 = (bf16[400,384]{1,0:T(8,128)(2,1)S(1)}, bf16[400,384]{1,0:T(8,128)(2,1)S(1)}, u32[]{:S(2)}, u32[]{:S(2)}) collective-permute-start(bf16[400,384]{1,0:T(8,128)(2,1)S(1)} %get-tuple-element.84), channel_id=1, source_target_pairs={{0,24},{1,25},{2,26},{3,27},{4,28},{5,29},{6,30},{7,31},{8,0},{9,1... | collective-permute-start | bytes 921608 | tf_op jit(solution)/shard_map/ppermute | solution.py:548
  72.0 0.8 attention_step.11
  72.8 3.9 %collective-permute-done.18.from_low = bf16[400,384]{1,0:T(8,128)(2,1)S(1)} collective-permute-done((bf16[400,384]{1,0:T(8,128)(2,1)S(1)}, bf16[400,384]{1,0:T(8,128)(2,1)S(1)}, u32[]{:S(2)}, u32[]{:S(2)}) %collective-permute-start.18) | collective-permute-done | bytes 307232 | tf_op jit(solution)/shard_map/ppermute | solution.py:548
  76.8 0.1 collective-permute-done.19.from_high
  76.9 0.8 finish.1
  77.7 0.1 collective-permute-start.20
  77.8 6.2 %collective-permute-start.21 = (bf16[1,128,384]{2,1,0:T(8,128)(2,1)S(1)}, bf16[1,128,384]{2,1,0:T(8,128)(2,1)S(1)}, u32[]{:S(2)}, u32[]{:S(2)}) collective-permute-start(bf16[1,128,384]{2,1,0:T(8,128)(2,1)S(1)} %get-tuple-element.91), channel_id=1, source_target_pairs={{0,31},{1,0},{2,1},{3,2},{4,3},{5,4},{6,5},{7,6},{8,7},{9,8},{10,9... | collective-permute-start | bytes 294920 | tf_op jit(solution)/shard_map/ppermute | solution.py:553
  83.9 2.2 %up_inner.1 = (bf16[6,192,256]{2,1,0:T(8,128)(2,1)}, f32[2,192,256]{2,1,0:T(8,128)S(1)}) custom-call(bf16[3,128,384]{2,1,0:T(8,128)(2,1)S(1)} %bitcast.11, bf16[2,2,2,768,256]{4,3,2,1,0:T(8,128)(2,1)S(1)} %up_phases.1._phases.weight, f32[8,1152]{1,0:T(8,128)S(1)} %pack.1.small), custom_call_target="tpu_custom_call" | custom-call | flops 792723456 | bytes 1000000 | tf_op jit(solution)/shard_map/up_inner/pallas_call | solution.py:44
  86.2 0.3 collective-permute-done.20.low
  86.4 1.2 %up_edges.1 = bf16[6,192,256]{2,1,0:T(8,128)(2,1)} custom-call(bf16[1,128,384]{2,1,0:T(8,128)(2,1)S(1)} %collective-permute-done.20.low, bf16[1,128,384]{2,1,0:T(8,128)(2,1)S(1)} %collective-permute-done.21.high, bf16[2,2,2,768,256]{4,3,2,1,0:T(8,128)(2,1)S(1)} %up_phases.1._phases.weight, ...), custom_call_target="tpu_custom_call", output_to_operand_aliasing={{}: (4, {})} | custom-call | flops 113246208 | bytes 1000000 | tf_op jit(solution)/shard_map/up_edges/pallas_call | solution.py:44
  (28 shorter events, 0.2 us)
Async XLA Ops:
  0.0 9.0 %collective-permute-start = (bf16[3,128,384]{2,1,0:T(8,128)(2,1)}, bf16[3,128,384]{2,1,0:T(8,128)(2,1)S(1)}, u32[]{:S(2)}, u32[]{:S(2)}) collective-permute-start(bf16[3,128,384]{2,1,0:T(8,128)(2,1)} %bitcast.6), channel_id=1, source_target_pairs={{0,64},{32,96},{64,128},{96,160},{128,192},{160,224},{192,0},{224,... | collective-permute-start | bytes 884744 | tf_op jit(solution)/shard_map/ppermute | solution.py:570
  2.1 1.0 %copy-start.1 = (bf16[1,3,128,384]{3,2,1,0:T(8,128)(2,1)S(1)}, bf16[1,3,128,384]{3,2,1,0:T(8,128)(2,1)}, u32[]{:S(2)}) copy-start(bf16[1,3,128,384]{3,2,1,0:T(8,128)(2,1)} %param.11) | copy-start | bytes 884740
  9.0 8.3 %collective-permute-start.3 = (bf16[3,128,384]{2,1,0:T(8,128)(2,1)S(1)}, bf16[3,128,384]{2,1,0:T(8,128)(2,1)S(1)}, u32[]{:S(2)}, u32[]{:S(2)}) collective-permute-start(bf16[3,128,384]{2,1,0:T(8,128)(2,1)S(1)} %get-tuple-element.53), channel_id=1, source_target_pairs={{0,32},{32,0},{64,96},{96,64},{128,160},{160,128},{192,224},{224,1... | collective-permute-start | bytes 884744 | tf_op jit(solution)/shard_map/ppermute | solution.py:590
  9.1 13.6 %collective-permute-start.1 = (bf16[2,128,384]{2,1,0:T(8,128)(2,1)S(1)}, bf16[2,128,384]{2,1,0:T(8,128)(2,1)S(1)}, u32[]{:S(2)}, u32[]{:S(2)}) collective-permute-start(bf16[2,128,384]{2,1,0:T(8,128)(2,1)S(1)} %get-tuple-element.51), channel_id=1, source_target_pairs={{0,1},{1,2},{2,3},{3,4},{4,5},{5,6},{6,7},{7,8},{8,9},{9,10},{10,1... | collective-permute-start | bytes 589832 | tf_op jit(solution)/shard_map/ppermute | solution.py:553
  11.1 11.6 %collective-permute-start.2 = (bf16[2,128,384]{2,1,0:T(8,128)(2,1)S(1)}, bf16[2,128,384]{2,1,0:T(8,128)(2,1)S(1)}, u32[]{:S(2)}, u32[]{:S(2)}) collective-permute-start(bf16[2,128,384]{2,1,0:T(8,128)(2,1)S(1)} %get-tuple-element.52), channel_id=1, source_target_pairs={{0,31},{1,0},{2,1},{3,2},{4,3},{5,4},{6,5},{7,6},{8,7},{9,8},{10,9... | collective-permute-start | bytes 589832 | tf_op jit(solution)/shard_map/ppermute | solution.py:553
  22.8 1.5 %collective-permute-start.4 = (bf16[2,128,384]{2,1,0:T(8,128)(2,1)S(1)}, bf16[2,128,384]{2,1,0:T(8,128)(2,1)S(1)}, u32[]{:S(2)}, u32[]{:S(2)}) collective-permute-start(bf16[2,128,384]{2,1,0:T(8,128)(2,1)S(1)} %pair_edges.1), channel_id=1, source_target_pairs={{0,32},{32,0},{64,96},{96,64},{128,160},{160,128},{192,224},{224,1... | collective-permute-start | bytes 589832 | tf_op jit(solution)/shard_map/ppermute | solution.py:601
  24.1 4.4 %copy-start = (bf16[384,1152]{1,0:T(8,128)(2,1)S(1)}, bf16[384,1152]{1,0:T(8,128)(2,1)}, u32[]{:S(2)}) copy-start(bf16[384,1152]{1,0:T(8,128)(2,1)} %weight.5) | copy-start | bytes 2654212
  25.2 10.5 %collective-permute-start.5 = (bf16[384,384]{1,0:T(8,128)(2,1)S(1)}, bf16[384,384]{1,0:T(8,128)(2,1)S(1)}, u32[]{:S(2)}, u32[]{:S(2)}) collective-permute-start(bf16[384,384]{1,0:T(8,128)(2,1)S(1)} %get-tuple-element.56.normed.refs_0_), channel_id=1, source_target_pairs={{0,1},{1,2},{2,3},{3,4},{4,5},{5,6},{6,7},{7,0},{8,9},{9,10},{10,1... | collective-permute-start | bytes 884744 | tf_op jit(solution)/shard_map/ppermute | solution.py:543
  25.2 10.4 %collective-permute-start.7 = (bf16[384,384]{1,0:T(8,128)(2,1)S(1)}, bf16[384,384]{1,0:T(8,128)(2,1)S(1)}, u32[]{:S(2)}, u32[]{:S(2)}) collective-permute-start(bf16[384,384]{1,0:T(8,128)(2,1)S(1)} %get-tuple-element.56.normed.refs_0_), channel_id=1, source_target_pairs={{0,7},{1,0},{2,1},{3,2},{4,3},{5,4},{6,5},{7,6},{8,15},{9,8},{10,9... | collective-permute-start | bytes 884744 | tf_op jit(solution)/shard_map/ppermute | solution.py:543
  29.2 11.5 %collective-permute-start.9 = (bf16[384,384]{1,0:T(8,128)(2,1)S(1)}, bf16[384,384]{1,0:T(8,128)(2,1)S(1)}, u32[]{:S(2)}, u32[]{:S(2)}) collective-permute-start(bf16[384,384]{1,0:T(8,128)(2,1)S(1)} %get-tuple-element.57.refs_5_.refs_4_), channel_id=1, source_target_pairs={{0,8},{1,9},{2,10},{3,11},{4,12},{5,13},{6,14},{7,15},{8,16},{9,17... | collective-permute-start | bytes 884744 | tf_op jit(solution)/shard_map/ppermute | solution.py:548
  29.2 11.4 %collective-permute-start.10 = (bf16[384,384]{1,0:T(8,128)(2,1)S(1)}, bf16[384,384]{1,0:T(8,128)(2,1)S(1)}, u32[]{:S(2)}, u32[]{:S(2)}) collective-permute-start(bf16[384,384]{1,0:T(8,128)(2,1)S(1)} %get-tuple-element.57.refs_5_.refs_4_), channel_id=1, source_target_pairs={{0,24},{1,25},{2,26},{3,27},{4,28},{5,29},{6,30},{7,31},{8,0},{9,1... | collective-permute-start | bytes 884744 | tf_op jit(solution)/shard_map/ppermute | solution.py:548
  35.7 9.6 %collective-permute-start.6 = (bf16[384,384]{1,0:T(8,128)(2,1)S(1)}, bf16[384,384]{1,0:T(8,128)(2,1)S(1)}, u32[]{:S(2)}, u32[]{:S(2)}) collective-permute-start(bf16[384,384]{1,0:T(8,128)(2,1)S(1)} %collective-permute-done.5.refs_1_), channel_id=1, source_target_pairs={{0,1},{1,2},{2,3},{3,4},{4,5},{5,6},{6,7},{7,0},{8,9},{9,10},{10,1... | collective-permute-start | bytes 884744 | tf_op jit(solution)/shard_map/ppermute | solution.py:543
  35.7 9.6 %collective-permute-start.8 = (bf16[384,384]{1,0:T(8,128)(2,1)S(1)}, bf16[384,384]{1,0:T(8,128)(2,1)S(1)}, u32[]{:S(2)}, u32[]{:S(2)}) collective-permute-start(bf16[384,384]{1,0:T(8,128)(2,1)S(1)} %collective-permute-done.7.refs_2_), channel_id=1, source_target_pairs={{0,7},{1,0},{2,1},{3,2},{4,3},{5,4},{6,5},{7,6},{8,15},{9,8},{10,9... | collective-permute-start | bytes 884744 | tf_op jit(solution)/shard_map/ppermute | solution.py:543
  38.9 9.6 %collective-permute-start.15 = (bf16[384,384]{1,0:T(8,128)(2,1)S(1)}, bf16[384,384]{1,0:T(8,128)(2,1)S(1)}, u32[]{:S(2)}, u32[]{:S(2)}) collective-permute-start(bf16[384,384]{1,0:T(8,128)(2,1)S(1)} %get-tuple-element.57.refs_5_.refs_4_), channel_id=1, source_target_pairs={{0,16},{1,17},{2,18},{3,19},{4,20},{5,21},{6,22},{7,23},{8,24},{9,... | collective-permute-start | bytes 884744 | tf_op jit(solution)/shard_map/ppermute | solution.py:548
  45.3 8.7 %collective-permute-start.11 = (bf16[384,384]{1,0:T(8,128)(2,1)S(1)}, bf16[384,384]{1,0:T(8,128)(2,1)S(1)}, u32[]{:S(2)}, u32[]{:S(2)}) collective-permute-start(bf16[384,384]{1,0:T(8,128)(2,1)S(1)} %get-tuple-element.59.refs_0_), channel_id=1, source_target_pairs={{0,1},{1,2},{2,3},{3,4},{4,5},{5,6},{6,7},{7,0},{8,9},{9,10},{10,1... | collective-permute-start | bytes 884744 | tf_op jit(solution)/shard_map/ppermute | solution.py:543
  45.3 8.8 %collective-permute-start.13 = (bf16[384,384]{1,0:T(8,128)(2,1)S(1)}, bf16[384,384]{1,0:T(8,128)(2,1)S(1)}, u32[]{:S(2)}, u32[]{:S(2)}) collective-permute-start(bf16[384,384]{1,0:T(8,128)(2,1)S(1)} %get-tuple-element.60.refs_1_), channel_id=1, source_target_pairs={{0,7},{1,0},{2,1},{3,2},{4,3},{5,4},{6,5},{7,6},{8,15},{9,8},{10,9... | collective-permute-start | bytes 884744 | tf_op jit(solution)/shard_map/ppermute | solution.py:543
  54.0 6.8 %collective-permute-start.12 = (bf16[192,384]{1,0:T(8,128)(2,1)S(1)}, bf16[192,384]{1,0:T(8,128)(2,1)S(1)}, u32[]{:S(2)}, u32[]{:S(2)}) collective-permute-start(bf16[192,384]{1,0:T(8,128)(2,1)S(1)} %slice.8), channel_id=1, source_target_pairs={{0,1},{1,2},{2,3},{3,4},{4,5},{5,6},{6,7},{7,0},{8,9},{9,10},{10,1... | collective-permute-start | bytes 442376 | tf_op jit(solution)/shard_map/ppermute | solution.py:543
  54.1 6.7 %collective-permute-start.14 = (bf16[192,384]{1,0:T(8,128)(2,1)S(1)}, bf16[192,384]{1,0:T(8,128)(2,1)S(1)}, u32[]{:S(2)}, u32[]{:S(2)}) collective-permute-start(bf16[192,384]{1,0:T(8,128)(2,1)S(1)} %slice.9), channel_id=1, source_target_pairs={{0,7},{1,0},{2,1},{3,2},{4,3},{5,4},{6,5},{7,6},{8,15},{9,8},{10,9... | collective-permute-start | bytes 442376 | tf_op jit(solution)/shard_map/ppermute | solution.py:543
  57.6 7.5 %copy-start.2 = (bf16[3,3,384,192]{2,3,1,0:T(8,128)(2,1)S(1)}, bf16[3,3,384,192]{2,3,1,0:T(8,128)(2,1)}, u32[]{:S(2)}) copy-start(bf16[3,3,384,192]{2,3,1,0:T(8,128)(2,1)} %param.20) | copy-start | bytes 3981316
  61.6 6.7 %collective-permute-start.16 = (bf16[208,384]{1,0:T(8,128)(2,1)S(1)}, bf16[208,384]{1,0:T(8,128)(2,1)S(1)}, u32[]{:S(2)}, u32[]{:S(2)}) collective-permute-start(bf16[208,384]{1,0:T(8,128)(2,1)S(1)} %get-tuple-element.75), channel_id=1, source_target_pairs={{0,8},{1,9},{2,10},{3,11},{4,12},{5,13},{6,14},{7,15},{8,16},{9,17... | collective-permute-start | bytes 479240 | tf_op jit(solution)/shard_map/ppermute | solution.py:548
  62.6 5.7 %collective-permute-start.17 = (bf16[208,384]{1,0:T(8,128)(2,1)S(1)}, bf16[208,384]{1,0:T(8,128)(2,1)S(1)}, u32[]{:S(2)}, u32[]{:S(2)}) collective-permute-start(bf16[208,384]{1,0:T(8,128)(2,1)S(1)} %get-tuple-element.76), channel_id=1, source_target_pairs={{0,24},{1,25},{2,26},{3,27},{4,28},{5,29},{6,30},{7,31},{8,0},{9,1... | collective-permute-start | bytes 479240 | tf_op jit(solution)/shard_map/ppermute | solution.py:548
  68.6 8.4 %copy-start.3 = (bf16[384,384]{1,0:T(8,128)(2,1)S(1)}, bf16[384,384]{1,0:T(8,128)(2,1)}, u32[]{:S(2)}) copy-start(bf16[384,384]{1,0:T(8,128)(2,1)} %wp.1) | copy-start | bytes 884740
  68.6 8.2 %collective-permute-start.18 = (bf16[400,384]{1,0:T(8,128)(2,1)S(1)}, bf16[400,384]{1,0:T(8,128)(2,1)S(1)}, u32[]{:S(2)}, u32[]{:S(2)}) collective-permute-start(bf16[400,384]{1,0:T(8,128)(2,1)S(1)} %get-tuple-element.83), channel_id=1, source_target_pairs={{0,8},{1,9},{2,10},{3,11},{4,12},{5,13},{6,14},{7,15},{8,16},{9,17... | collective-permute-start | bytes 921608 | tf_op jit(solution)/shard_map/ppermute | solution.py:548
  70.1 6.9 %collective-permute-start.19 = (bf16[400,384]{1,0:T(8,128)(2,1)S(1)}, bf16[400,384]{1,0:T(8,128)(2,1)S(1)}, u32[]{:S(2)}, u32[]{:S(2)}) collective-permute-start(bf16[400,384]{1,0:T(8,128)(2,1)S(1)} %get-tuple-element.84), channel_id=1, source_target_pairs={{0,24},{1,25},{2,26},{3,27},{4,28},{5,29},{6,30},{7,31},{8,0},{9,1... | collective-permute-start | bytes 921608 | tf_op jit(solution)/shard_map/ppermute | solution.py:548
  77.7 8.8 %collective-permute-start.20 = (bf16[1,128,384]{2,1,0:T(8,128)(2,1)S(1)}, bf16[1,128,384]{2,1,0:T(8,128)(2,1)S(1)}, u32[]{:S(2)}, u32[]{:S(2)}) collective-permute-start(bf16[1,128,384]{2,1,0:T(8,128)(2,1)S(1)} %get-tuple-element.90), channel_id=1, source_target_pairs={{0,1},{1,2},{2,3},{3,4},{4,5},{5,6},{6,7},{7,8},{8,9},{9,10},{10,1... | collective-permute-start | bytes 294920 | tf_op jit(solution)/shard_map/ppermute | solution.py:553
  77.8 8.7 %collective-permute-start.21 = (bf16[1,128,384]{2,1,0:T(8,128)(2,1)S(1)}, bf16[1,128,384]{2,1,0:T(8,128)(2,1)S(1)}, u32[]{:S(2)}, u32[]{:S(2)}) collective-permute-start(bf16[1,128,384]{2,1,0:T(8,128)(2,1)S(1)} %get-tuple-element.91), channel_id=1, source_target_pairs={{0,31},{1,0},{2,1},{3,2},{4,3},{5,4},{6,5},{7,6},{8,7},{9,8},{10,9... | collective-permute-start | bytes 294920 | tf_op jit(solution)/shard_map/ppermute | solution.py:553

commit v2 on v0

--- a/solution.py
+++ b/solution.py
@@ -418,7 +418,7 @@
     return top + jnp.log2(total), out
 
 
-def relay_kernel(from_low, from_high, m, total, acc, _phases, to_low, to_high):
+def relay_kernel(from_low, from_high, m, total, acc, to_low, to_high):
     for side, got, out in ((0, from_high, to_low), (1, from_low, to_high)):
         cols = slice(side * CELLS, (side + 1) * CELLS)
         stat = m[:, cols] + jnp.log2(total[:, cols])
@@ -435,7 +435,7 @@
         out[C:] = stat_rows([stat_t, stat_b])
 
 
-def finish_kernel(from_low, from_high, m, total, acc, shift, weight, wp, small, block, out):
+def finish_kernel(from_low, from_high, m, total, acc, shift, weight, wp, small, block, _phases, out):
     c = shift[...]
     stat = m[...] + jnp.log2(total[...]) + c
     mine = acc[...] / total[...]
@@ -664,9 +664,7 @@
         half_low,
         half_high,
         *sides,
-        phases,
         name="relay",
-        specs=[VM] * 5 + [ANY],
     )
     from_low, from_high = permute_x(to_high, 1), permute_x(to_low, -1)
     (mine,) = attention_step(last, near, (state,), 2 * CELLS, 3 * CELLS)
@@ -681,7 +679,9 @@
         proj_weight,
         small,
         block,
+        phases,
         name="finish",
+        specs=[VM] * 10 + [ANY],
         flops=4 * CELLS * C * C,
     ).reshape(ROWS, W, C)
     edge_low, edge_high = to_bands(attended[2:], 1), to_bands(attended[:1], -1)

time: 88 us -> 88 us (level)
  no operation moved by 1% of the time
where the time goes in v2:
time: 88 us; the launch traced here: 87.8 us
  starting transfers between devices  41.4 us (47%)
  Pallas kernels  31 us (35%)
  waiting for transfers between devices  13.3 us (15%)
  local copies, waits for them, and re-layouts  1.03 us (1%)
    pallas_call x21, Pallas kernels, call(): pl.pallas_call(body, in_specs=specs or [VM] * len(args), out_specs=[out_s...  31 us
    ppermute x4, starting transfers between devices, to_bands(): return lax.ppermute(value, 'rows', [(i, (i + by) % n) for i in range(n)])  14.5 us
    ppermute x8, starting transfers between devices, permute_z(): return lax.ppermute(value, 'rows', pairs)  13.4 us
    ppermute x7, starting transfers between devices, permute_x(): return lax.ppermute(value, 'rows', pairs)  12.1 us
    ppermute x8, waiting for transfers between devices, permute_z(): return lax.ppermute(value, 'rows', pairs)  5.31 us
    ppermute x7, waiting for transfers between devices, permute_x(): return lax.ppermute(value, 'rows', pairs)  5.2 us
  transfers between devices with their start and end apart: 22, of which 10 were waited for; matrix products, arithmetic and copies ran while one was open for 1% of the time, Pallas kernels for 31%

profile of v2, /device:TPU:16, one launch (start us, length us, event | category | flops | bytes accessed | tf_op | source)
XLA Modules:
  0.0 87.8 jit_solution(4918588741932708031)
XLA Ops:
  0.0 1.3 %collective-permute-start = (bf16[3,128,384]{2,1,0:T(8,128)(2,1)}, bf16[3,128,384]{2,1,0:T(8,128)(2,1)S(1)}, u32[]{:S(2)}, u32[]{:S(2)}) collective-permute-start(bf16[3,128,384]{2,1,0:T(8,128)(2,1)} %bitcast.10), channel_id=1, source_target_pairs={{0,64},{32,96},{64,128},{96,160},{128,192},{160,224},{192,0},{224,... | collective-permute-start | bytes 884744 | tf_op jit(solution)/shard_map/ppermute | solution.py:567
  1.3 0.8 pad_add_fusion.flat
  2.1 1.0 %copy-done.1 = bf16[1,3,128,384]{3,2,1,0:T(8,128)(2,1)S(1)} copy-done((bf16[1,3,128,384]{3,2,1,0:T(8,128)(2,1)S(1)}, bf16[1,3,128,384]{3,2,1,0:T(8,128)(2,1)}, u32[]{:S(2)}) %copy-start.1) | copy-done | bytes 294936
  3.0 4.2 %conv_own.1 = (f32[384,384]{1,0:T(8,128)S(1)}, bf16[2,3,384,384]{3,2,1,0:T(8,128)(2,1)S(1)}, bf16[2,3,3,384,384]{4,3,2,1,0:T(8,128)(2,1)S(1)}) custom-call(bf16[3,128,384]{2,1,0:T(8,128)(2,1)S(1)} %bitcast.11, f32[8,1152]{1,0:T(8,128)S(1)} %pack.1.small, bf16[3,3,3,384,384]{4,3,2,1,0:T(8,128)(2,1)} %weight.3), custom_call_target="tpu_custom_call" | custom-call | flops 1019215872 | bytes 1000000 | tf_op jit(solution)/shard_map/conv_own/pallas_call | solution.py:44
  7.2 1.7 %collective-permute-done.two = bf16[3,128,384]{2,1,0:T(8,128)(2,1)S(1)} collective-permute-done((bf16[3,128,384]{2,1,0:T(8,128)(2,1)}, bf16[3,128,384]{2,1,0:T(8,128)(2,1)S(1)}, u32[]{:S(2)}, u32[]{:S(2)}) %collective-permute-start) | collective-permute-done | bytes 294944 | tf_op jit(solution)/shard_map/ppermute | solution.py:567
  9.0 0.1 collective-permute-start.3
  9.1 2.0 %collective-permute-start.1 = (bf16[2,128,384]{2,1,0:T(8,128)(2,1)S(1)}, bf16[2,128,384]{2,1,0:T(8,128)(2,1)S(1)}, u32[]{:S(2)}, u32[]{:S(2)}) collective-permute-start(bf16[2,128,384]{2,1,0:T(8,128)(2,1)S(1)} %get-tuple-element.48), channel_id=1, source_target_pairs={{0,1},{1,2},{2,3},{3,4},{4,5},{5,6},{6,7},{7,8},{8,9},{9,10},{10,1... | collective-permute-start | bytes 589832 | tf_op jit(solution)/shard_map/ppermute | solution.py:550
  11.1 6.2 %collective-permute-start.2 = (bf16[2,128,384]{2,1,0:T(8,128)(2,1)S(1)}, bf16[2,128,384]{2,1,0:T(8,128)(2,1)S(1)}, u32[]{:S(2)}, u32[]{:S(2)}) collective-permute-start(bf16[2,128,384]{2,1,0:T(8,128)(2,1)S(1)} %get-tuple-element.49), channel_id=1, source_target_pairs={{0,31},{1,0},{2,1},{3,2},{4,3},{5,4},{6,5},{7,6},{8,7},{9,8},{10,9... | collective-permute-start | bytes 589832 | tf_op jit(solution)/shard_map/ppermute | solution.py:550
  17.4 4.9 %conv_earlier.1._acc.start = f32[384,384]{1,0:T(8,128)S(1)} custom-call(bf16[3,128,384]{2,1,0:T(8,128)(2,1)S(1)} %collective-permute-done.two, bf16[3,128,384]{2,1,0:T(8,128)(2,1)S(1)} %collective-permute-done.3.one, f32[8,1152]{1,0:T(8,128)S(1)} %pack.1.small, ...), custom_call_target="tpu_custom_call", output_to_operand_aliasing={{}: (4, {})} | custom-call | flops 2038431744 | bytes 1000000 | tf_op jit(solution)/shard_map/conv_earlier/pallas_call | solution.py:44
  22.2 0.5 collective-permute-done.1.low
  22.8 0.1 collective-permute-start.4
  22.9 1.2 %conv_edges.1.start = f32[384,384]{1,0:T(8,128)S(1)} custom-call(bf16[2,128,384]{2,1,0:T(8,128)(2,1)S(1)} %collective-permute-done.1.low, bf16[2,128,384]{2,1,0:T(8,128)(2,1)S(1)} %collective-permute-done.2.high, f32[8,1152]{1,0:T(8,128)S(1)} %pack.1.small, bf16[2,3,384,384]{3,2,1,0:T(8,128)(2,1)S(1)} %get-tuple-element.52.w_own, ...), custom_call_target="tpu_custom_call", output_to_operand_aliasing={{}: (5, {})} | custom-call | flops 226492416 | bytes 1000000 | tf_op jit(solution)/shard_map/conv_edges/pallas_call | solution.py:44
  24.1 0.2 collective-permute-done.4.edges
  24.3 0.9 conv_last.1
  25.2 0.1 collective-permute-start.5
  25.2 3.2 %collective-permute-start.7 = (bf16[384,384]{1,0:T(8,128)(2,1)S(1)}, bf16[384,384]{1,0:T(8,128)(2,1)S(1)}, u32[]{:S(2)}, u32[]{:S(2)}) collective-permute-start(bf16[384,384]{1,0:T(8,128)(2,1)S(1)} %get-tuple-element.53.normed.refs_0_), channel_id=1, source_target_pairs={{0,7},{1,0},{2,1},{3,2},{4,3},{5,4},{6,5},{7,6},{8,15},{9,8},{10,9... | collective-permute-start | bytes 884744 | tf_op jit(solution)/shard_map/ppermute | solution.py:540
  28.5 0.7 queries.1
  29.2 3.2 %collective-permute-start.10 = (bf16[384,384]{1,0:T(8,128)(2,1)S(1)}, bf16[384,384]{1,0:T(8,128)(2,1)S(1)}, u32[]{:S(2)}, u32[]{:S(2)}) collective-permute-start(bf16[384,384]{1,0:T(8,128)(2,1)S(1)} %get-tuple-element.54.refs_5_.refs_4_), channel_id=1, source_target_pairs={{0,24},{1,25},{2,26},{3,27},{4,28},{5,29},{6,30},{7,31},{8,0},{9,1... | collective-permute-start | bytes 884744 | tf_op jit(solution)/shard_map/ppermute | solution.py:545
  32.5 3.2 %collective-permute-done.5.refs_1_ = bf16[384,384]{1,0:T(8,128)(2,1)S(1)} collective-permute-done((bf16[384,384]{1,0:T(8,128)(2,1)S(1)}, bf16[384,384]{1,0:T(8,128)(2,1)S(1)}, u32[]{:S(2)}, u32[]{:S(2)}) %collective-permute-start.5) | collective-permute-done | bytes 294944 | tf_op jit(solution)/shard_map/ppermute | solution.py:540
  35.7 3.2 %collective-permute-start.8 = (bf16[384,384]{1,0:T(8,128)(2,1)S(1)}, bf16[384,384]{1,0:T(8,128)(2,1)S(1)}, u32[]{:S(2)}, u32[]{:S(2)}) collective-permute-start(bf16[384,384]{1,0:T(8,128)(2,1)S(1)} %collective-permute-done.7.refs_2_), channel_id=1, source_target_pairs={{0,7},{1,0},{2,1},{3,2},{4,3},{5,4},{6,5},{7,6},{8,15},{9,8},{10,9... | collective-permute-start | bytes 884744 | tf_op jit(solution)/shard_map/ppermute | solution.py:540
  38.9 1.7 %collective-permute-start.15 = (bf16[384,384]{1,0:T(8,128)(2,1)S(1)}, bf16[384,384]{1,0:T(8,128)(2,1)S(1)}, u32[]{:S(2)}, u32[]{:S(2)}) collective-permute-start(bf16[384,384]{1,0:T(8,128)(2,1)S(1)} %get-tuple-element.54.refs_5_.refs_4_), channel_id=1, source_target_pairs={{0,16},{1,17},{2,18},{3,19},{4,20},{5,21},{6,22},{7,23},{8,24},{9,... | collective-permute-start | bytes 884744 | tf_op jit(solution)/shard_map/ppermute | solution.py:545
  40.6 3.2 %attention_step.6 = (f32[1,1152]{1,0:T(1,128)S(1)}, f32[1,1152]{1,0:T(1,128)S(1)}, f32[384,1152]{1,0:T(8,128)S(1)}) custom-call(bf16[384,384]{1,0:T(8,128)(2,1)S(1)} %get-tuple-element.53.normed.refs_0_, bf16[384,384]{1,0:T(8,128)(2,1)S(1)} %collective-permute-done.5.refs_1_, bf16[384,384]{1,0:T(8,128)(2,1)S(1)} %collective-permute-done.7.refs_2_, ...), custom_call_target="tpu_custom_call" | custom-call | flops 2038431744 | bytes 6000000 | tf_op jit(solution)/shard_map/attention_step/pallas_call | solution.py:44
  43.9 1.4 %collective-permute-done.6.refs_0_ = bf16[384,384]{1,0:T(8,128)(2,1)S(1)} collective-permute-done((bf16[384,384]{1,0:T(8,128)(2,1)S(1)}, bf16[384,384]{1,0:T(8,128)(2,1)S(1)}, u32[]{:S(2)}, u32[]{:S(2)}) %collective-permute-start.6) | collective-permute-done | bytes 294944 | tf_op jit(solution)/shard_map/ppermute | solution.py:540
  45.3 3.2 %collective-permute-start.13 = (bf16[384,384]{1,0:T(8,128)(2,1)S(1)}, bf16[384,384]{1,0:T(8,128)(2,1)S(1)}, u32[]{:S(2)}, u32[]{:S(2)}) collective-permute-start(bf16[384,384]{1,0:T(8,128)(2,1)S(1)} %get-tuple-element.57.refs_1_), channel_id=1, source_target_pairs={{0,7},{1,0},{2,1},{3,2},{4,3},{5,4},{6,5},{7,6},{8,15},{9,8},{10,9... | collective-permute-start | bytes 884744 | tf_op jit(solution)/shard_map/ppermute | solution.py:540
  48.5 1.6 %attention_step.7 = (f32[1,384]{1,0:T(1,128)S(1)}, f32[1,384]{1,0:T(1,128)S(1)}, f32[384,384]{1,0:T(8,128)S(1)}) custom-call(bf16[384,384]{1,0:T(8,128)(2,1)S(1)} %get-tuple-element.53.normed.refs_0_, bf16[384,384]{1,0:T(8,128)(2,1)S(1)} %collective-permute-done.5.refs_1_, bf16[384,384]{1,0:T(8,128)(2,1)S(1)} %collective-permute-done.7.refs_2_, ...), custom_call_target="tpu_custom_call" | custom-call | flops 679477248 | bytes 6000000 | tf_op jit(solution)/shard_map/attention_step/pallas_call | solution.py:44
  50.1 3.2 %attention_step.8 = (f32[1,1152]{1,0:T(1,128)S(1)}, f32[1,1152]{1,0:T(1,128)S(1)}, f32[384,1152]{1,0:T(8,128)S(1)}, f32[1,384]{1,0:T(1,128)S(1)}, f32[1,384]{1,0:T(1,128)S(1)}, /*index=5*/f32[384,384]{1,0:T(8,128)S(1)}) custom-call(bf16[384,384]{1,0:T(8,128)(2,1)S(1)} %get-tuple-element., ...), custom_call_target="tpu_custom_call", output_to_operand_aliasing={{0}: (6, {}), {1}: (7, {}), {2}: (8, {}), {3}: (9, {}), {4}... | custom-call | flops 1811939328 | bytes 6000000 | tf_op jit(solution)/shard_map/attention_step/pallas_call | solution.py:44
  53.3 0.7 collective-permute-done.11.refs_0_
  54.0 0.1 collective-permute-start.12
  54.1 3.5 %collective-permute-start.14 = (bf16[192,384]{1,0:T(8,128)(2,1)S(1)}, bf16[192,384]{1,0:T(8,128)(2,1)S(1)}, u32[]{:S(2)}, u32[]{:S(2)}) collective-permute-start(bf16[192,384]{1,0:T(8,128)(2,1)S(1)} %slice.25), channel_id=1, source_target_pairs={{0,7},{1,0},{2,1},{3,2},{4,3},{5,4},{6,5},{7,6},{8,15},{9,8},{10,9... | collective-permute-start | bytes 442376 | tf_op jit(solution)/shard_map/ppermute | solution.py:540
  57.6 3.1 %attention_step.9 = (f32[1,1152]{1,0:T(1,128)S(1)}, f32[1,1152]{1,0:T(1,128)S(1)}, f32[384,1152]{1,0:T(8,128)S(1)}, f32[1,384]{1,0:T(1,128)S(1)}, f32[1,384]{1,0:T(1,128)S(1)}, /*index=5*/f32[384,384]{1,0:T(8,128)S(1)}) custom-call(bf16[384,384]{1,0:T(8,128)(2,1)S(1)} %collective-permute, ...), custom_call_target="tpu_custom_call", output_to_operand_aliasing={{0}: (6, {}), {1}: (7, {}), {2}: (8, {}), {3}: (9, {}), {4}... | custom-call | flops 1811939328 | bytes 6000000 | tf_op jit(solution)/shard_map/attention_step/pallas_call | solution.py:44
  60.8 0.8 opposite.1
  61.6 1.0 %collective-permute-start.16 = (bf16[208,384]{1,0:T(8,128)(2,1)S(1)}, bf16[208,384]{1,0:T(8,128)(2,1)S(1)}, u32[]{:S(2)}, u32[]{:S(2)}) collective-permute-start(bf16[208,384]{1,0:T(8,128)(2,1)S(1)} %get-tuple-element.72), channel_id=1, source_target_pairs={{0,8},{1,9},{2,10},{3,11},{4,12},{5,13},{6,14},{7,15},{8,16},{9,17... | collective-permute-start | bytes 479240 | tf_op jit(solution)/shard_map/ppermute | solution.py:545
  62.6 2.6 %collective-permute-start.17 = (bf16[208,384]{1,0:T(8,128)(2,1)S(1)}, bf16[208,384]{1,0:T(8,128)(2,1)S(1)}, u32[]{:S(2)}, u32[]{:S(2)}) collective-permute-start(bf16[208,384]{1,0:T(8,128)(2,1)S(1)} %get-tuple-element.73), channel_id=1, source_target_pairs={{0,24},{1,25},{2,26},{3,27},{4,28},{5,29},{6,30},{7,31},{8,0},{9,1... | collective-permute-start | bytes 479240 | tf_op jit(solution)/shard_map/ppermute | solution.py:545
  65.1 1.0 %attention_step.10 = (f32[1,768]{1,0:T(1,128)S(1)}, f32[1,768]{1,0:T(1,128)S(1)}, f32[384,768]{1,0:T(8,128)S(1)}) custom-call(bf16[192,384]{1,0:T(8,128)(2,1)S(1)} %collective-permute-done.12.refs_0_, bf16[192,384]{1,0:T(8,128)(2,1)S(1)} %collective-permute-done.14.refs_1_, bf16[384,384]{1,0:T(8,128)(2,1)S(1)} %collective-permute-done.9.refs_3_.refs_2_, ...), custom_call_target="tpu_custom_call" | custom-call | flops 452984832 | bytes 6000000 | tf_op jit(solution)/shard_map/attention_step/pallas_call | solution.py:44
  66.2 2.1 %collective-permute-done.16.from_low = bf16[208,384]{1,0:T(8,128)(2,1)S(1)} collective-permute-done((bf16[208,384]{1,0:T(8,128)(2,1)S(1)}, bf16[208,384]{1,0:T(8,128)(2,1)S(1)}, u32[]{:S(2)}, u32[]{:S(2)}) %collective-permute-start.16) | collective-permute-done | bytes 159776 | tf_op jit(solution)/shard_map/ppermute | solution.py:545
  68.3 0.2 relay.1
  68.6 1.5 %collective-permute-start.18 = (bf16[400,384]{1,0:T(8,128)(2,1)S(1)}, bf16[400,384]{1,0:T(8,128)(2,1)S(1)}, u32[]{:S(2)}, u32[]{:S(2)}) collective-permute-start(bf16[400,384]{1,0:T(8,128)(2,1)S(1)} %get-tuple-element.80), channel_id=1, source_target_pairs={{0,8},{1,9},{2,10},{3,11},{4,12},{5,13},{6,14},{7,15},{8,16},{9,17... | collective-permute-start | bytes 921608 | tf_op jit(solution)/shard_map/ppermute | solution.py:545
  70.0 2.0 %collective-permute-start.19 = (bf16[400,384]{1,0:T(8,128)(2,1)S(1)}, bf16[400,384]{1,0:T(8,128)(2,1)S(1)}, u32[]{:S(2)}, u32[]{:S(2)}) collective-permute-start(bf16[400,384]{1,0:T(8,128)(2,1)S(1)} %get-tuple-element.81), channel_id=1, source_target_pairs={{0,24},{1,25},{2,26},{3,27},{4,28},{5,29},{6,30},{7,31},{8,0},{9,1... | collective-permute-start | bytes 921608 | tf_op jit(solution)/shard_map/ppermute | solution.py:545
  72.0 1.0 %up_phases.1._phases.weight = bf16[2,2,2,768,256]{4,3,2,1,0:T(8,128)(2,1)S(1)} custom-call(bf16[3,3,192,384]{3,2,1,0:T(8,128)(2,1)S(1)} %bitcast.15), custom_call_target="tpu_custom_call" | custom-call | flops 10000000 | bytes 4000000 | tf_op jit(solution)/shard_map/up_phases/pallas_call | solution.py:44
  73.0 0.8 attention_step.11
  73.8 2.9 %collective-permute-done.18.from_low = bf16[400,384]{1,0:T(8,128)(2,1)S(1)} collective-permute-done((bf16[400,384]{1,0:T(8,128)(2,1)S(1)}, bf16[400,384]{1,0:T(8,128)(2,1)S(1)}, u32[]{:S(2)}, u32[]{:S(2)}) %collective-permute-start.18) | collective-permute-done | bytes 307232 | tf_op jit(solution)/shard_map/ppermute | solution.py:545
  76.8 0.1 collective-permute-done.19.from_high
  76.9 0.7 finish.1
  77.7 0.1 collective-permute-start.20
  77.8 6.2 %collective-permute-start.21 = (bf16[1,128,384]{2,1,0:T(8,128)(2,1)S(1)}, bf16[1,128,384]{2,1,0:T(8,128)(2,1)S(1)}, u32[]{:S(2)}, u32[]{:S(2)}) collective-permute-start(bf16[1,128,384]{2,1,0:T(8,128)(2,1)S(1)} %get-tuple-element.89), channel_id=1, source_target_pairs={{0,31},{1,0},{2,1},{3,2},{4,3},{5,4},{6,5},{7,6},{8,7},{9,8},{10,9... | collective-permute-start | bytes 294920 | tf_op jit(solution)/shard_map/ppermute | solution.py:550
  83.9 2.2 %up_inner.1 = (bf16[6,192,256]{2,1,0:T(8,128)(2,1)}, f32[2,192,256]{2,1,0:T(8,128)S(1)}) custom-call(bf16[3,128,384]{2,1,0:T(8,128)(2,1)S(1)} %bitcast.14, bf16[2,2,2,768,256]{4,3,2,1,0:T(8,128)(2,1)S(1)} %up_phases.1._phases.weight, f32[8,1152]{1,0:T(8,128)S(1)} %pack.1.small), custom_call_target="tpu_custom_call" | custom-call | flops 792723456 | bytes 1000000 | tf_op jit(solution)/shard_map/up_inner/pallas_call | solution.py:44
  86.2 0.3 collective-permute-done.20.low
  86.5 1.2 %up_edges.1 = bf16[6,192,256]{2,1,0:T(8,128)(2,1)} custom-call(bf16[1,128,384]{2,1,0:T(8,128)(2,1)S(1)} %collective-permute-done.20.low, bf16[1,128,384]{2,1,0:T(8,128)(2,1)S(1)} %collective-permute-done.21.high, bf16[2,2,2,768,256]{4,3,2,1,0:T(8,128)(2,1)S(1)} %up_phases.1._phases.weight, ...), custom_call_target="tpu_custom_call", output_to_operand_aliasing={{}: (4, {})} | custom-call | flops 113246208 | bytes 1000000 | tf_op jit(solution)/shard_map/up_edges/pallas_call | solution.py:44
  (29 shorter events, 0.3 us)
Async XLA Ops:
  0.0 9.0 %collective-permute-start = (bf16[3,128,384]{2,1,0:T(8,128)(2,1)}, bf16[3,128,384]{2,1,0:T(8,128)(2,1)S(1)}, u32[]{:S(2)}, u32[]{:S(2)}) collective-permute-start(bf16[3,128,384]{2,1,0:T(8,128)(2,1)} %bitcast.10), channel_id=1, source_target_pairs={{0,64},{32,96},{64,128},{96,160},{128,192},{160,224},{192,0},{224,... | collective-permute-start | bytes 884744 | tf_op jit(solution)/shard_map/ppermute | solution.py:567
  2.1 1.0 %copy-start.1 = (bf16[1,3,128,384]{3,2,1,0:T(8,128)(2,1)S(1)}, bf16[1,3,128,384]{3,2,1,0:T(8,128)(2,1)}, u32[]{:S(2)}) copy-start(bf16[1,3,128,384]{3,2,1,0:T(8,128)(2,1)} %param.11) | copy-start | bytes 884740
  9.0 8.3 %collective-permute-start.3 = (bf16[3,128,384]{2,1,0:T(8,128)(2,1)S(1)}, bf16[3,128,384]{2,1,0:T(8,128)(2,1)S(1)}, u32[]{:S(2)}, u32[]{:S(2)}) collective-permute-start(bf16[3,128,384]{2,1,0:T(8,128)(2,1)S(1)} %get-tuple-element.50), channel_id=1, source_target_pairs={{0,32},{32,0},{64,96},{96,64},{128,160},{160,128},{192,224},{224,1... | collective-permute-start | bytes 884744 | tf_op jit(solution)/shard_map/ppermute | solution.py:587
  9.1 13.6 %collective-permute-start.1 = (bf16[2,128,384]{2,1,0:T(8,128)(2,1)S(1)}, bf16[2,128,384]{2,1,0:T(8,128)(2,1)S(1)}, u32[]{:S(2)}, u32[]{:S(2)}) collective-permute-start(bf16[2,128,384]{2,1,0:T(8,128)(2,1)S(1)} %get-tuple-element.48), channel_id=1, source_target_pairs={{0,1},{1,2},{2,3},{3,4},{4,5},{5,6},{6,7},{7,8},{8,9},{9,10},{10,1... | collective-permute-start | bytes 589832 | tf_op jit(solution)/shard_map/ppermute | solution.py:550
  11.1 11.6 %collective-permute-start.2 = (bf16[2,128,384]{2,1,0:T(8,128)(2,1)S(1)}, bf16[2,128,384]{2,1,0:T(8,128)(2,1)S(1)}, u32[]{:S(2)}, u32[]{:S(2)}) collective-permute-start(bf16[2,128,384]{2,1,0:T(8,128)(2,1)S(1)} %get-tuple-element.49), channel_id=1, source_target_pairs={{0,31},{1,0},{2,1},{3,2},{4,3},{5,4},{6,5},{7,6},{8,7},{9,8},{10,9... | collective-permute-start | bytes 589832 | tf_op jit(solution)/shard_map/ppermute | solution.py:550
  22.8 1.5 %collective-permute-start.4 = (bf16[2,128,384]{2,1,0:T(8,128)(2,1)S(1)}, bf16[2,128,384]{2,1,0:T(8,128)(2,1)S(1)}, u32[]{:S(2)}, u32[]{:S(2)}) collective-permute-start(bf16[2,128,384]{2,1,0:T(8,128)(2,1)S(1)} %pair_edges.1), channel_id=1, source_target_pairs={{0,32},{32,0},{64,96},{96,64},{128,160},{160,128},{192,224},{224,1... | collective-permute-start | bytes 589832 | tf_op jit(solution)/shard_map/ppermute | solution.py:598
  24.1 4.4 %copy-start = (bf16[384,1152]{1,0:T(8,128)(2,1)S(1)}, bf16[384,1152]{1,0:T(8,128)(2,1)}, u32[]{:S(2)}) copy-start(bf16[384,1152]{1,0:T(8,128)(2,1)} %weight.5) | copy-start | bytes 2654212
  25.2 10.5 %collective-permute-start.5 = (bf16[384,384]{1,0:T(8,128)(2,1)S(1)}, bf16[384,384]{1,0:T(8,128)(2,1)S(1)}, u32[]{:S(2)}, u32[]{:S(2)}) collective-permute-start(bf16[384,384]{1,0:T(8,128)(2,1)S(1)} %get-tuple-element.53.normed.refs_0_), channel_id=1, source_target_pairs={{0,1},{1,2},{2,3},{3,4},{4,5},{5,6},{6,7},{7,0},{8,9},{9,10},{10,1... | collective-permute-start | bytes 884744 | tf_op jit(solution)/shard_map/ppermute | solution.py:540
  25.2 10.4 %collective-permute-start.7 = (bf16[384,384]{1,0:T(8,128)(2,1)S(1)}, bf16[384,384]{1,0:T(8,128)(2,1)S(1)}, u32[]{:S(2)}, u32[]{:S(2)}) collective-permute-start(bf16[384,384]{1,0:T(8,128)(2,1)S(1)} %get-tuple-element.53.normed.refs_0_), channel_id=1, source_target_pairs={{0,7},{1,0},{2,1},{3,2},{4,3},{5,4},{6,5},{7,6},{8,15},{9,8},{10,9... | collective-permute-start | bytes 884744 | tf_op jit(solution)/shard_map/ppermute | solution.py:540
  29.2 11.5 %collective-permute-start.9 = (bf16[384,384]{1,0:T(8,128)(2,1)S(1)}, bf16[384,384]{1,0:T(8,128)(2,1)S(1)}, u32[]{:S(2)}, u32[]{:S(2)}) collective-permute-start(bf16[384,384]{1,0:T(8,128)(2,1)S(1)} %get-tuple-element.54.refs_5_.refs_4_), channel_id=1, source_target_pairs={{0,8},{1,9},{2,10},{3,11},{4,12},{5,13},{6,14},{7,15},{8,16},{9,17... | collective-permute-start | bytes 884744 | tf_op jit(solution)/shard_map/ppermute | solution.py:545
  29.2 11.4 %collective-permute-start.10 = (bf16[384,384]{1,0:T(8,128)(2,1)S(1)}, bf16[384,384]{1,0:T(8,128)(2,1)S(1)}, u32[]{:S(2)}, u32[]{:S(2)}) collective-permute-start(bf16[384,384]{1,0:T(8,128)(2,1)S(1)} %get-tuple-element.54.refs_5_.refs_4_), channel_id=1, source_target_pairs={{0,24},{1,25},{2,26},{3,27},{4,28},{5,29},{6,30},{7,31},{8,0},{9,1... | collective-permute-start | bytes 884744 | tf_op jit(solution)/shard_map/ppermute | solution.py:545
  35.7 9.6 %collective-permute-start.6 = (bf16[384,384]{1,0:T(8,128)(2,1)S(1)}, bf16[384,384]{1,0:T(8,128)(2,1)S(1)}, u32[]{:S(2)}, u32[]{:S(2)}) collective-permute-start(bf16[384,384]{1,0:T(8,128)(2,1)S(1)} %collective-permute-done.5.refs_1_), channel_id=1, source_target_pairs={{0,1},{1,2},{2,3},{3,4},{4,5},{5,6},{6,7},{7,0},{8,9},{9,10},{10,1... | collective-permute-start | bytes 884744 | tf_op jit(solution)/shard_map/ppermute | solution.py:540
  35.7 9.6 %collective-permute-start.8 = (bf16[384,384]{1,0:T(8,128)(2,1)S(1)}, bf16[384,384]{1,0:T(8,128)(2,1)S(1)}, u32[]{:S(2)}, u32[]{:S(2)}) collective-permute-start(bf16[384,384]{1,0:T(8,128)(2,1)S(1)} %collective-permute-done.7.refs_2_), channel_id=1, source_target_pairs={{0,7},{1,0},{2,1},{3,2},{4,3},{5,4},{6,5},{7,6},{8,15},{9,8},{10,9... | collective-permute-start | bytes 884744 | tf_op jit(solution)/shard_map/ppermute | solution.py:540
  38.9 9.6 %collective-permute-start.15 = (bf16[384,384]{1,0:T(8,128)(2,1)S(1)}, bf16[384,384]{1,0:T(8,128)(2,1)S(1)}, u32[]{:S(2)}, u32[]{:S(2)}) collective-permute-start(bf16[384,384]{1,0:T(8,128)(2,1)S(1)} %get-tuple-element.54.refs_5_.refs_4_), channel_id=1, source_target_pairs={{0,16},{1,17},{2,18},{3,19},{4,20},{5,21},{6,22},{7,23},{8,24},{9,... | collective-permute-start | bytes 884744 | tf_op jit(solution)/shard_map/ppermute | solution.py:545
  45.3 8.7 %collective-permute-start.11 = (bf16[384,384]{1,0:T(8,128)(2,1)S(1)}, bf16[384,384]{1,0:T(8,128)(2,1)S(1)}, u32[]{:S(2)}, u32[]{:S(2)}) collective-permute-start(bf16[384,384]{1,0:T(8,128)(2,1)S(1)} %get-tuple-element.56.refs_0_), channel_id=1, source_target_pairs={{0,1},{1,2},{2,3},{3,4},{4,5},{5,6},{6,7},{7,0},{8,9},{9,10},{10,1... | collective-permute-start | bytes 884744 | tf_op jit(solution)/shard_map/ppermute | solution.py:540
  45.3 8.8 %collective-permute-start.13 = (bf16[384,384]{1,0:T(8,128)(2,1)S(1)}, bf16[384,384]{1,0:T(8,128)(2,1)S(1)}, u32[]{:S(2)}, u32[]{:S(2)}) collective-permute-start(bf16[384,384]{1,0:T(8,128)(2,1)S(1)} %get-tuple-element.57.refs_1_), channel_id=1, source_target_pairs={{0,7},{1,0},{2,1},{3,2},{4,3},{5,4},{6,5},{7,6},{8,15},{9,8},{10,9... | collective-permute-start | bytes 884744 | tf_op jit(solution)/shard_map/ppermute | solution.py:540
  54.0 6.8 %collective-permute-start.12 = (bf16[192,384]{1,0:T(8,128)(2,1)S(1)}, bf16[192,384]{1,0:T(8,128)(2,1)S(1)}, u32[]{:S(2)}, u32[]{:S(2)}) collective-permute-start(bf16[192,384]{1,0:T(8,128)(2,1)S(1)} %slice.24), channel_id=1, source_target_pairs={{0,1},{1,2},{2,3},{3,4},{4,5},{5,6},{6,7},{7,0},{8,9},{9,10},{10,1... | collective-permute-start | bytes 442376 | tf_op jit(solution)/shard_map/ppermute | solution.py:540
  54.1 6.7 %collective-permute-start.14 = (bf16[192,384]{1,0:T(8,128)(2,1)S(1)}, bf16[192,384]{1,0:T(8,128)(2,1)S(1)}, u32[]{:S(2)}, u32[]{:S(2)}) collective-permute-start(bf16[192,384]{1,0:T(8,128)(2,1)S(1)} %slice.25), channel_id=1, source_target_pairs={{0,7},{1,0},{2,1},{3,2},{4,3},{5,4},{6,5},{7,6},{8,15},{9,8},{10,9... | collective-permute-start | bytes 442376 | tf_op jit(solution)/shard_map/ppermute | solution.py:540
  61.6 6.7 %collective-permute-start.16 = (bf16[208,384]{1,0:T(8,128)(2,1)S(1)}, bf16[208,384]{1,0:T(8,128)(2,1)S(1)}, u32[]{:S(2)}, u32[]{:S(2)}) collective-permute-start(bf16[208,384]{1,0:T(8,128)(2,1)S(1)} %get-tuple-element.72), channel_id=1, source_target_pairs={{0,8},{1,9},{2,10},{3,11},{4,12},{5,13},{6,14},{7,15},{8,16},{9,17... | collective-permute-start | bytes 479240 | tf_op jit(solution)/shard_map/ppermute | solution.py:545
  62.6 5.7 %collective-permute-start.17 = (bf16[208,384]{1,0:T(8,128)(2,1)S(1)}, bf16[208,384]{1,0:T(8,128)(2,1)S(1)}, u32[]{:S(2)}, u32[]{:S(2)}) collective-permute-start(bf16[208,384]{1,0:T(8,128)(2,1)S(1)} %get-tuple-element.73), channel_id=1, source_target_pairs={{0,24},{1,25},{2,26},{3,27},{4,28},{5,29},{6,30},{7,31},{8,0},{9,1... | collective-permute-start | bytes 479240 | tf_op jit(solution)/shard_map/ppermute | solution.py:545
  65.1 6.9 %copy-start.2 = (bf16[3,3,384,192]{2,3,1,0:T(8,128)(2,1)S(1)}, bf16[3,3,384,192]{2,3,1,0:T(8,128)(2,1)}, u32[]{:S(2)}) copy-start(bf16[3,3,384,192]{2,3,1,0:T(8,128)(2,1)} %param.20) | copy-start | bytes 3981316
  68.6 8.2 %collective-permute-start.18 = (bf16[400,384]{1,0:T(8,128)(2,1)S(1)}, bf16[400,384]{1,0:T(8,128)(2,1)S(1)}, u32[]{:S(2)}, u32[]{:S(2)}) collective-permute-start(bf16[400,384]{1,0:T(8,128)(2,1)S(1)} %get-tuple-element.80), channel_id=1, source_target_pairs={{0,8},{1,9},{2,10},{3,11},{4,12},{5,13},{6,14},{7,15},{8,16},{9,17... | collective-permute-start | bytes 921608 | tf_op jit(solution)/shard_map/ppermute | solution.py:545
  70.0 6.9 %collective-permute-start.19 = (bf16[400,384]{1,0:T(8,128)(2,1)S(1)}, bf16[400,384]{1,0:T(8,128)(2,1)S(1)}, u32[]{:S(2)}, u32[]{:S(2)}) collective-permute-start(bf16[400,384]{1,0:T(8,128)(2,1)S(1)} %get-tuple-element.81), channel_id=1, source_target_pairs={{0,24},{1,25},{2,26},{3,27},{4,28},{5,29},{6,30},{7,31},{8,0},{9,1... | collective-permute-start | bytes 921608 | tf_op jit(solution)/shard_map/ppermute | solution.py:545
  73.0 3.9 %copy-start.3 = (bf16[384,384]{1,0:T(8,128)(2,1)S(1)}, bf16[384,384]{1,0:T(8,128)(2,1)}, u32[]{:S(2)}) copy-start(bf16[384,384]{1,0:T(8,128)(2,1)} %wp.1) | copy-start | bytes 884740
  77.7 8.8 %collective-permute-start.20 = (bf16[1,128,384]{2,1,0:T(8,128)(2,1)S(1)}, bf16[1,128,384]{2,1,0:T(8,128)(2,1)S(1)}, u32[]{:S(2)}, u32[]{:S(2)}) collective-permute-start(bf16[1,128,384]{2,1,0:T(8,128)(2,1)S(1)} %get-tuple-element.90), channel_id=1, source_target_pairs={{0,1},{1,2},{2,3},{3,4},{4,5},{5,6},{6,7},{7,8},{8,9},{9,10},{10,1... | collective-permute-start | bytes 294920 | tf_op jit(solution)/shard_map/ppermute | solution.py:550
  77.8 8.7 %collective-permute-start.21 = (bf16[1,128,384]{2,1,0:T(8,128)(2,1)S(1)}, bf16[1,128,384]{2,1,0:T(8,128)(2,1)S(1)}, u32[]{:S(2)}, u32[]{:S(2)}) collective-permute-start(bf16[1,128,384]{2,1,0:T(8,128)(2,1)S(1)} %get-tuple-element.89), channel_id=1, source_target_pairs={{0,31},{1,0},{2,1},{3,2},{4,3},{5,4},{6,5},{7,6},{8,7},{9,8},{10,9... | collective-permute-start | bytes 294920 | tf_op jit(solution)/shard_map/ppermute | solution.py:550

commit v3 on v0

--- a/solution.py
+++ b/solution.py
@@ -147,33 +147,29 @@
     )
 
 
-def conv_earlier_kernel(two, one, small, weight, start, acc, scratch):
-    has_two, has_one, _, _ = inside()
-    band_rows(scratch, 0, two, small[0:1, :C], has_two)
-    band_rows(scratch, 1, one, small[0:1, :C], has_one)
+def conv_earlier_kernel(time_tap, frame, small, weight, start, acc, scratch):
+    band_rows(scratch, 0, frame, small[0:1, :C], inside()[time_tap])
     acc[...] = start[...]
 
-    def step(g, carry):
-        t, b = g // 3, g % 3
-        acc[...] += band_tap(scratch, t, b, weight[t, b])
+    def step(b, carry):
+        acc[...] += band_tap(scratch, 0, b, weight[time_tap, b])
         return carry
 
-    lax.fori_loop(0, 6, step, 0)
-
-
-def conv_earlier(two, one, small, weight, start):
+    lax.fori_loop(0, 3, step, 0)
+
+
+def conv_earlier(frame, small, weight, time_tap, start):
     return call(
-        conv_earlier_kernel,
+        functools.partial(conv_earlier_kernel, time_tap),
         [((CELLS, C), F32)],
-        two,
-        one,
+        frame,
         small,
         weight,
         start,
         name="conv_earlier",
-        flops=2 * CELLS * 18 * C * C,
-        scratch=[pltpu.VMEM((2, ROWS + 2, W, 3 * C), BF16)],
-        aliases={4: 0},
+        flops=2 * CELLS * 9 * C * C,
+        scratch=[pltpu.VMEM((1, ROWS + 2, W, 3 * C), BF16)],
+        aliases={3: 0},
     )
 
 
@@ -585,7 +581,8 @@
     )
     low, high = to_bands(to_next, 1), to_bands(to_previous, -1)
     one = lax.ppermute(pair, "tm", pairs)
-    acc = conv_earlier(two, one, small, w_pair, acc)
+    acc = conv_earlier(two, small, w_pair, 0, acc)
+    acc = conv_earlier(one, small, w_pair, 1, acc)
     pair_edges = call(
         pair_edges_kernel,
         [((2, W, C), BF16)],

time: 88 us -> 88 us (level)
    pallas_call x21 -> x22, Pallas kernels: 31 us -> 31.1 us  [call(): pl.pallas_call(body, in_specs=specs or [VM] * len(args), out_specs=[out_s...]
where the time goes in v3:
time: 88 us; the launch traced here: 87.8 us
  starting transfers between devices  41.3 us (47%)
  Pallas kernels  31.1 us (35%)
  waiting for transfers between devices  13.1 us (15%)
  local copies, waits for them, and re-layouts  1.03 us (1%)
    pallas_call x22, Pallas kernels, call(): pl.pallas_call(body, in_specs=specs or [VM] * len(args), out_specs=[out_s...  31.1 us
    ppermute x4, starting transfers between devices, to_bands(): return lax.ppermute(value, 'rows', [(i, (i + by) % n) for i in range(n)])  14.5 us
    ppermute x8, starting transfers between devices, permute_z(): return lax.ppermute(value, 'rows', pairs)  13.4 us
    ppermute x7, starting transfers between devices, permute_x(): return lax.ppermute(value, 'rows', pairs)  12 us
    ppermute x8, waiting for transfers between devices, permute_z(): return lax.ppermute(value, 'rows', pairs)  5.31 us
    ppermute x7, waiting for transfers between devices, permute_x(): return lax.ppermute(value, 'rows', pairs)  5.2 us
  transfers between devices with their start and end apart: 22, of which 10 were waited for; matrix products, arithmetic and copies ran while one was open for 1% of the time, Pallas kernels for 31%

profile of v3, /device:TPU:16, one launch (start us, length us, event | category | flops | bytes accessed | tf_op | source)
XLA Modules:
  0.0 87.8 jit_solution(8512095086712433855)
XLA Ops:
  0.0 1.3 %collective-permute-start = (bf16[3,128,384]{2,1,0:T(8,128)(2,1)}, bf16[3,128,384]{2,1,0:T(8,128)(2,1)S(1)}, u32[]{:S(2)}, u32[]{:S(2)}) collective-permute-start(bf16[3,128,384]{2,1,0:T(8,128)(2,1)} %bitcast.10), channel_id=1, source_target_pairs={{0,64},{32,96},{64,128},{96,160},{128,192},{160,224},{192,0},{224,... | collective-permute-start | bytes 884744 | tf_op jit(solution)/shard_map/ppermute | solution.py:563
  1.3 0.8 pad_add_fusion.flat
  2.1 1.0 %copy-done.1 = bf16[1,3,128,384]{3,2,1,0:T(8,128)(2,1)S(1)} copy-done((bf16[1,3,128,384]{3,2,1,0:T(8,128)(2,1)S(1)}, bf16[1,3,128,384]{3,2,1,0:T(8,128)(2,1)}, u32[]{:S(2)}) %copy-start.1) | copy-done | bytes 294936
  3.0 4.2 %conv_own.1 = (f32[384,384]{1,0:T(8,128)S(1)}, bf16[2,3,384,384]{3,2,1,0:T(8,128)(2,1)S(1)}, bf16[2,3,3,384,384]{4,3,2,1,0:T(8,128)(2,1)S(1)}) custom-call(bf16[3,128,384]{2,1,0:T(8,128)(2,1)S(1)} %bitcast.11, f32[8,1152]{1,0:T(8,128)S(1)} %pack.1.small, bf16[3,3,3,384,384]{4,3,2,1,0:T(8,128)(2,1)} %weight.3), custom_call_target="tpu_custom_call" | custom-call | flops 1019215872 | bytes 1000000 | tf_op jit(solution)/shard_map/conv_own/pallas_call | solution.py:44
  7.2 1.7 %collective-permute-done.two.frame = bf16[3,128,384]{2,1,0:T(8,128)(2,1)S(1)} collective-permute-done((bf16[3,128,384]{2,1,0:T(8,128)(2,1)}, bf16[3,128,384]{2,1,0:T(8,128)(2,1)S(1)}, u32[]{:S(2)}, u32[]{:S(2)}) %collective-permute-start) | collective-permute-done | bytes 294944 | tf_op jit(solution)/shard_map/ppermute | solution.py:563
  9.0 0.1 collective-permute-start.3
  9.1 2.0 %collective-permute-start.1 = (bf16[2,128,384]{2,1,0:T(8,128)(2,1)S(1)}, bf16[2,128,384]{2,1,0:T(8,128)(2,1)S(1)}, u32[]{:S(2)}, u32[]{:S(2)}) collective-permute-start(bf16[2,128,384]{2,1,0:T(8,128)(2,1)S(1)} %get-tuple-element.48), channel_id=1, source_target_pairs={{0,1},{1,2},{2,3},{3,4},{4,5},{5,6},{6,7},{7,8},{8,9},{9,10},{10,1... | collective-permute-start | bytes 589832 | tf_op jit(solution)/shard_map/ppermute | solution.py:546
  11.1 6.2 %collective-permute-start.2 = (bf16[2,128,384]{2,1,0:T(8,128)(2,1)S(1)}, bf16[2,128,384]{2,1,0:T(8,128)(2,1)S(1)}, u32[]{:S(2)}, u32[]{:S(2)}) collective-permute-start(bf16[2,128,384]{2,1,0:T(8,128)(2,1)S(1)} %get-tuple-element.49), channel_id=1, source_target_pairs={{0,31},{1,0},{2,1},{3,2},{4,3},{5,4},{6,5},{7,6},{8,7},{9,8},{10,9... | collective-permute-start | bytes 589832 | tf_op jit(solution)/shard_map/ppermute | solution.py:546
  17.3 2.5 %conv_earlier.2.start = f32[384,384]{1,0:T(8,128)S(1)} custom-call(bf16[3,128,384]{2,1,0:T(8,128)(2,1)S(1)} %collective-permute-done.two.frame, f32[8,1152]{1,0:T(8,128)S(1)} %pack.1.small, bf16[2,3,3,384,384]{4,3,2,1,0:T(8,128)(2,1)S(1)} %get-tuple-element.51.weight.w_pair, f32[384,384]{1,0:T(8,128)S(1)} %get-tuple-element.47._acc.start), custom_call_target="tpu_custom_call", output_to_operand_aliasing={{}: (3, {})} | custom-call | flops 1019215872 | bytes 1000000 | tf_op jit(solution)/shard_map/conv_earlier/pallas_call | solution.py:44
  19.9 2.5 %conv_earlier.3._acc.start = f32[384,384]{1,0:T(8,128)S(1)} custom-call(bf16[3,128,384]{2,1,0:T(8,128)(2,1)S(1)} %collective-permute-done.3.frame, f32[8,1152]{1,0:T(8,128)S(1)} %pack.1.small, bf16[2,3,3,384,384]{4,3,2,1,0:T(8,128)(2,1)S(1)} %get-tuple-element.51.weight.w_pair, f32[384,384]{1,0:T(8,128)S(1)} %conv_earlier.2.start), custom_call_target="tpu_custom_call", output_to_operand_aliasing={{}: (3, {})} | custom-call | flops 1019215872 | bytes 1000000 | tf_op jit(solution)/shard_map/conv_earlier/pallas_call | solution.py:44
  22.4 0.4 collective-permute-done.1.low
  22.8 0.1 collective-permute-start.4
  22.9 1.2 %conv_edges.1.start = f32[384,384]{1,0:T(8,128)S(1)} custom-call(bf16[2,128,384]{2,1,0:T(8,128)(2,1)S(1)} %collective-permute-done.1.low, bf16[2,128,384]{2,1,0:T(8,128)(2,1)S(1)} %collective-permute-done.2.high, f32[8,1152]{1,0:T(8,128)S(1)} %pack.1.small, bf16[2,3,384,384]{3,2,1,0:T(8,128)(2,1)S(1)} %get-tuple-element.52.w_own, ...), custom_call_target="tpu_custom_call", output_to_operand_aliasing={{}: (5, {})} | custom-call | flops 226492416 | bytes 1000000 | tf_op jit(solution)/shard_map/conv_edges/pallas_call | solution.py:44
  24.1 0.2 collective-permute-done.4.edges
  24.3 0.9 conv_last.1
  25.2 0.1 collective-permute-start.5
  25.2 3.2 %collective-permute-start.7 = (bf16[384,384]{1,0:T(8,128)(2,1)S(1)}, bf16[384,384]{1,0:T(8,128)(2,1)S(1)}, u32[]{:S(2)}, u32[]{:S(2)}) collective-permute-start(bf16[384,384]{1,0:T(8,128)(2,1)S(1)} %get-tuple-element.53.normed.refs_0_), channel_id=1, source_target_pairs={{0,7},{1,0},{2,1},{3,2},{4,3},{5,4},{6,5},{7,6},{8,15},{9,8},{10,9... | collective-permute-start | bytes 884744 | tf_op jit(solution)/shard_map/ppermute | solution.py:536
  28.5 0.7 queries.1
  29.2 3.2 %collective-permute-start.10 = (bf16[384,384]{1,0:T(8,128)(2,1)S(1)}, bf16[384,384]{1,0:T(8,128)(2,1)S(1)}, u32[]{:S(2)}, u32[]{:S(2)}) collective-permute-start(bf16[384,384]{1,0:T(8,128)(2,1)S(1)} %get-tuple-element.54.refs_5_.refs_4_), channel_id=1, source_target_pairs={{0,24},{1,25},{2,26},{3,27},{4,28},{5,29},{6,30},{7,31},{8,0},{9,1... | collective-permute-start | bytes 884744 | tf_op jit(solution)/shard_map/ppermute | solution.py:541
  32.5 3.2 %collective-permute-done.5.refs_1_ = bf16[384,384]{1,0:T(8,128)(2,1)S(1)} collective-permute-done((bf16[384,384]{1,0:T(8,128)(2,1)S(1)}, bf16[384,384]{1,0:T(8,128)(2,1)S(1)}, u32[]{:S(2)}, u32[]{:S(2)}) %collective-permute-start.5) | collective-permute-done | bytes 294944 | tf_op jit(solution)/shard_map/ppermute | solution.py:536
  35.7 3.2 %collective-permute-start.8 = (bf16[384,384]{1,0:T(8,128)(2,1)S(1)}, bf16[384,384]{1,0:T(8,128)(2,1)S(1)}, u32[]{:S(2)}, u32[]{:S(2)}) collective-permute-start(bf16[384,384]{1,0:T(8,128)(2,1)S(1)} %collective-permute-done.7.refs_2_), channel_id=1, source_target_pairs={{0,7},{1,0},{2,1},{3,2},{4,3},{5,4},{6,5},{7,6},{8,15},{9,8},{10,9... | collective-permute-start | bytes 884744 | tf_op jit(solution)/shard_map/ppermute | solution.py:536
  38.9 1.7 %collective-permute-start.15 = (bf16[384,384]{1,0:T(8,128)(2,1)S(1)}, bf16[384,384]{1,0:T(8,128)(2,1)S(1)}, u32[]{:S(2)}, u32[]{:S(2)}) collective-permute-start(bf16[384,384]{1,0:T(8,128)(2,1)S(1)} %get-tuple-element.54.refs_5_.refs_4_), channel_id=1, source_target_pairs={{0,16},{1,17},{2,18},{3,19},{4,20},{5,21},{6,22},{7,23},{8,24},{9,... | collective-permute-start | bytes 884744 | tf_op jit(solution)/shard_map/ppermute | solution.py:541
  40.6 3.2 %attention_step.6 = (f32[1,1152]{1,0:T(1,128)S(1)}, f32[1,1152]{1,0:T(1,128)S(1)}, f32[384,1152]{1,0:T(8,128)S(1)}) custom-call(bf16[384,384]{1,0:T(8,128)(2,1)S(1)} %get-tuple-element.53.normed.refs_0_, bf16[384,384]{1,0:T(8,128)(2,1)S(1)} %collective-permute-done.5.refs_1_, bf16[384,384]{1,0:T(8,128)(2,1)S(1)} %collective-permute-done.7.refs_2_, ...), custom_call_target="tpu_custom_call" | custom-call | flops 2038431744 | bytes 6000000 | tf_op jit(solution)/shard_map/attention_step/pallas_call | solution.py:44
  43.9 1.4 %collective-permute-done.6.refs_0_ = bf16[384,384]{1,0:T(8,128)(2,1)S(1)} collective-permute-done((bf16[384,384]{1,0:T(8,128)(2,1)S(1)}, bf16[384,384]{1,0:T(8,128)(2,1)S(1)}, u32[]{:S(2)}, u32[]{:S(2)}) %collective-permute-start.6) | collective-permute-done | bytes 294944 | tf_op jit(solution)/shard_map/ppermute | solution.py:536
  45.3 3.2 %collective-permute-start.13 = (bf16[384,384]{1,0:T(8,128)(2,1)S(1)}, bf16[384,384]{1,0:T(8,128)(2,1)S(1)}, u32[]{:S(2)}, u32[]{:S(2)}) collective-permute-start(bf16[384,384]{1,0:T(8,128)(2,1)S(1)} %get-tuple-element.57.refs_1_), channel_id=1, source_target_pairs={{0,7},{1,0},{2,1},{3,2},{4,3},{5,4},{6,5},{7,6},{8,15},{9,8},{10,9... | collective-permute-start | bytes 884744 | tf_op jit(solution)/shard_map/ppermute | solution.py:536
  48.5 1.6 %attention_step.7 = (f32[1,384]{1,0:T(1,128)S(1)}, f32[1,384]{1,0:T(1,128)S(1)}, f32[384,384]{1,0:T(8,128)S(1)}) custom-call(bf16[384,384]{1,0:T(8,128)(2,1)S(1)} %get-tuple-element.53.normed.refs_0_, bf16[384,384]{1,0:T(8,128)(2,1)S(1)} %collective-permute-done.5.refs_1_, bf16[384,384]{1,0:T(8,128)(2,1)S(1)} %collective-permute-done.7.refs_2_, ...), custom_call_target="tpu_custom_call" | custom-call | flops 679477248 | bytes 6000000 | tf_op jit(solution)/shard_map/attention_step/pallas_call | solution.py:44
  50.1 3.2 %attention_step.8 = (f32[1,1152]{1,0:T(1,128)S(1)}, f32[1,1152]{1,0:T(1,128)S(1)}, f32[384,1152]{1,0:T(8,128)S(1)}, f32[1,384]{1,0:T(1,128)S(1)}, f32[1,384]{1,0:T(1,128)S(1)}, /*index=5*/f32[384,384]{1,0:T(8,128)S(1)}) custom-call(bf16[384,384]{1,0:T(8,128)(2,1)S(1)} %get-tuple-element., ...), custom_call_target="tpu_custom_call", output_to_operand_aliasing={{0}: (6, {}), {1}: (7, {}), {2}: (8, {}), {3}: (9, {}), {4}... | custom-call | flops 1811939328 | bytes 6000000 | tf_op jit(solution)/shard_map/attention_step/pallas_call | solution.py:44
  53.3 0.7 collective-permute-done.11.refs_0_
  54.0 0.1 collective-permute-start.12
  54.1 3.5 %collective-permute-start.14 = (bf16[192,384]{1,0:T(8,128)(2,1)S(1)}, bf16[192,384]{1,0:T(8,128)(2,1)S(1)}, u32[]{:S(2)}, u32[]{:S(2)}) collective-permute-start(bf16[192,384]{1,0:T(8,128)(2,1)S(1)} %slice.25), channel_id=1, source_target_pairs={{0,7},{1,0},{2,1},{3,2},{4,3},{5,4},{6,5},{7,6},{8,15},{9,8},{10,9... | collective-permute-start | bytes 442376 | tf_op jit(solution)/shard_map/ppermute | solution.py:536
  57.6 3.2 %attention_step.9 = (f32[1,1152]{1,0:T(1,128)S(1)}, f32[1,1152]{1,0:T(1,128)S(1)}, f32[384,1152]{1,0:T(8,128)S(1)}, f32[1,384]{1,0:T(1,128)S(1)}, f32[1,384]{1,0:T(1,128)S(1)}, /*index=5*/f32[384,384]{1,0:T(8,128)S(1)}) custom-call(bf16[384,384]{1,0:T(8,128)(2,1)S(1)} %collective-permute, ...), custom_call_target="tpu_custom_call", output_to_operand_aliasing={{0}: (6, {}), {1}: (7, {}), {2}: (8, {}), {3}: (9, {}), {4}... | custom-call | flops 1811939328 | bytes 6000000 | tf_op jit(solution)/shard_map/attention_step/pallas_call | solution.py:44
  60.8 0.8 opposite.1
  61.6 1.0 %collective-permute-start.16 = (bf16[208,384]{1,0:T(8,128)(2,1)S(1)}, bf16[208,384]{1,0:T(8,128)(2,1)S(1)}, u32[]{:S(2)}, u32[]{:S(2)}) collective-permute-start(bf16[208,384]{1,0:T(8,128)(2,1)S(1)} %get-tuple-element.72), channel_id=1, source_target_pairs={{0,8},{1,9},{2,10},{3,11},{4,12},{5,13},{6,14},{7,15},{8,16},{9,17... | collective-permute-start | bytes 479240 | tf_op jit(solution)/shard_map/ppermute | solution.py:541
  62.6 2.5 %collective-permute-start.17 = (bf16[208,384]{1,0:T(8,128)(2,1)S(1)}, bf16[208,384]{1,0:T(8,128)(2,1)S(1)}, u32[]{:S(2)}, u32[]{:S(2)}) collective-permute-start(bf16[208,384]{1,0:T(8,128)(2,1)S(1)} %get-tuple-element.73), channel_id=1, source_target_pairs={{0,24},{1,25},{2,26},{3,27},{4,28},{5,29},{6,30},{7,31},{8,0},{9,1... | collective-permute-start | bytes 479240 | tf_op jit(solution)/shard_map/ppermute | solution.py:541
  65.1 1.0 %up_phases.1._phases.weight = bf16[2,2,2,768,256]{4,3,2,1,0:T(8,128)(2,1)S(1)} custom-call(bf16[3,3,192,384]{3,2,1,0:T(8,128)(2,1)S(1)} %bitcast.15), custom_call_target="tpu_custom_call" | custom-call | flops 10000000 | bytes 4000000 | tf_op jit(solution)/shard_map/up_phases/pallas_call | solution.py:44
  66.1 1.0 %attention_step.10 = (f32[1,768]{1,0:T(1,128)S(1)}, f32[1,768]{1,0:T(1,128)S(1)}, f32[384,768]{1,0:T(8,128)S(1)}) custom-call(bf16[192,384]{1,0:T(8,128)(2,1)S(1)} %collective-permute-done.12.refs_0_, bf16[192,384]{1,0:T(8,128)(2,1)S(1)} %collective-permute-done.14.refs_1_, bf16[384,384]{1,0:T(8,128)(2,1)S(1)} %collective-permute-done.9.refs_3_.refs_2_, ...), custom_call_target="tpu_custom_call" | custom-call | flops 452984832 | bytes 6000000 | tf_op jit(solution)/shard_map/attention_step/pallas_call | solution.py:44
  67.2 1.1 %collective-permute-done.16.from_low = bf16[208,384]{1,0:T(8,128)(2,1)S(1)} collective-permute-done((bf16[208,384]{1,0:T(8,128)(2,1)S(1)}, bf16[208,384]{1,0:T(8,128)(2,1)S(1)}, u32[]{:S(2)}, u32[]{:S(2)}) %collective-permute-start.16) | collective-permute-done | bytes 159776 | tf_op jit(solution)/shard_map/ppermute | solution.py:541
  68.3 0.2 relay.1
  68.6 1.5 %collective-permute-start.18 = (bf16[400,384]{1,0:T(8,128)(2,1)S(1)}, bf16[400,384]{1,0:T(8,128)(2,1)S(1)}, u32[]{:S(2)}, u32[]{:S(2)}) collective-permute-start(bf16[400,384]{1,0:T(8,128)(2,1)S(1)} %get-tuple-element.80), channel_id=1, source_target_pairs={{0,8},{1,9},{2,10},{3,11},{4,12},{5,13},{6,14},{7,15},{8,16},{9,17... | collective-permute-start | bytes 921608 | tf_op jit(solution)/shard_map/ppermute | solution.py:541
  70.0 2.0 %collective-permute-start.19 = (bf16[400,384]{1,0:T(8,128)(2,1)S(1)}, bf16[400,384]{1,0:T(8,128)(2,1)S(1)}, u32[]{:S(2)}, u32[]{:S(2)}) collective-permute-start(bf16[400,384]{1,0:T(8,128)(2,1)S(1)} %get-tuple-element.81), channel_id=1, source_target_pairs={{0,24},{1,25},{2,26},{3,27},{4,28},{5,29},{6,30},{7,31},{8,0},{9,1... | collective-permute-start | bytes 921608 | tf_op jit(solution)/shard_map/ppermute | solution.py:541
  72.0 0.8 attention_step.11
  72.8 3.9 %collective-permute-done.18.from_low = bf16[400,384]{1,0:T(8,128)(2,1)S(1)} collective-permute-done((bf16[400,384]{1,0:T(8,128)(2,1)S(1)}, bf16[400,384]{1,0:T(8,128)(2,1)S(1)}, u32[]{:S(2)}, u32[]{:S(2)}) %collective-permute-start.18) | collective-permute-done | bytes 307232 | tf_op jit(solution)/shard_map/ppermute | solution.py:541
  76.8 0.1 collective-permute-done.19.from_high
  76.9 0.8 finish.1
  77.8 6.2 %collective-permute-start.21 = (bf16[1,128,384]{2,1,0:T(8,128)(2,1)S(1)}, bf16[1,128,384]{2,1,0:T(8,128)(2,1)S(1)}, u32[]{:S(2)}, u32[]{:S(2)}) collective-permute-start(bf16[1,128,384]{2,1,0:T(8,128)(2,1)S(1)} %get-tuple-element.89), channel_id=1, source_target_pairs={{0,31},{1,0},{2,1},{3,2},{4,3},{5,4},{6,5},{7,6},{8,7},{9,8},{10,9... | collective-permute-start | bytes 294920 | tf_op jit(solution)/shard_map/ppermute | solution.py:546
  84.0 2.2 %up_inner.1 = (bf16[6,192,256]{2,1,0:T(8,128)(2,1)}, f32[2,192,256]{2,1,0:T(8,128)S(1)}) custom-call(bf16[3,128,384]{2,1,0:T(8,128)(2,1)S(1)} %bitcast.14, bf16[2,2,2,768,256]{4,3,2,1,0:T(8,128)(2,1)S(1)} %up_phases.1._phases.weight, f32[8,1152]{1,0:T(8,128)S(1)} %pack.1.small), custom_call_target="tpu_custom_call" | custom-call | flops 792723456 | bytes 1000000 | tf_op jit(solution)/shard_map/up_inner/pallas_call | solution.py:44
  86.2 0.3 collective-permute-done.20.low
  86.5 1.2 %up_edges.1 = bf16[6,192,256]{2,1,0:T(8,128)(2,1)} custom-call(bf16[1,128,384]{2,1,0:T(8,128)(2,1)S(1)} %collective-permute-done.20.low, bf16[1,128,384]{2,1,0:T(8,128)(2,1)S(1)} %collective-permute-done.21.high, bf16[2,2,2,768,256]{4,3,2,1,0:T(8,128)(2,1)S(1)} %up_phases.1._phases.weight, ...), custom_call_target="tpu_custom_call", output_to_operand_aliasing={{}: (4, {})} | custom-call | flops 113246208 | bytes 1000000 | tf_op jit(solution)/shard_map/up_edges/pallas_call | solution.py:44
  (30 shorter events, 0.3 us)
Async XLA Ops:
  0.0 9.0 %collective-permute-start = (bf16[3,128,384]{2,1,0:T(8,128)(2,1)}, bf16[3,128,384]{2,1,0:T(8,128)(2,1)S(1)}, u32[]{:S(2)}, u32[]{:S(2)}) collective-permute-start(bf16[3,128,384]{2,1,0:T(8,128)(2,1)} %bitcast.10), channel_id=1, source_target_pairs={{0,64},{32,96},{64,128},{96,160},{128,192},{160,224},{192,0},{224,... | collective-permute-start | bytes 884744 | tf_op jit(solution)/shard_map/ppermute | solution.py:563
  2.1 1.0 %copy-start.1 = (bf16[1,3,128,384]{3,2,1,0:T(8,128)(2,1)S(1)}, bf16[1,3,128,384]{3,2,1,0:T(8,128)(2,1)}, u32[]{:S(2)}) copy-start(bf16[1,3,128,384]{3,2,1,0:T(8,128)(2,1)} %param.11) | copy-start | bytes 884740
  9.0 10.8 %collective-permute-start.3 = (bf16[3,128,384]{2,1,0:T(8,128)(2,1)S(1)}, bf16[3,128,384]{2,1,0:T(8,128)(2,1)S(1)}, u32[]{:S(2)}, u32[]{:S(2)}) collective-permute-start(bf16[3,128,384]{2,1,0:T(8,128)(2,1)S(1)} %get-tuple-element.50), channel_id=1, source_target_pairs={{0,32},{32,0},{64,96},{96,64},{128,160},{160,128},{192,224},{224,1... | collective-permute-start | bytes 884744 | tf_op jit(solution)/shard_map/ppermute | solution.py:583
  9.1 13.6 %collective-permute-start.1 = (bf16[2,128,384]{2,1,0:T(8,128)(2,1)S(1)}, bf16[2,128,384]{2,1,0:T(8,128)(2,1)S(1)}, u32[]{:S(2)}, u32[]{:S(2)}) collective-permute-start(bf16[2,128,384]{2,1,0:T(8,128)(2,1)S(1)} %get-tuple-element.48), channel_id=1, source_target_pairs={{0,1},{1,2},{2,3},{3,4},{4,5},{5,6},{6,7},{7,8},{8,9},{9,10},{10,1... | collective-permute-start | bytes 589832 | tf_op jit(solution)/shard_map/ppermute | solution.py:546
  11.1 11.6 %collective-permute-start.2 = (bf16[2,128,384]{2,1,0:T(8,128)(2,1)S(1)}, bf16[2,128,384]{2,1,0:T(8,128)(2,1)S(1)}, u32[]{:S(2)}, u32[]{:S(2)}) collective-permute-start(bf16[2,128,384]{2,1,0:T(8,128)(2,1)S(1)} %get-tuple-element.49), channel_id=1, source_target_pairs={{0,31},{1,0},{2,1},{3,2},{4,3},{5,4},{6,5},{7,6},{8,7},{9,8},{10,9... | collective-permute-start | bytes 589832 | tf_op jit(solution)/shard_map/ppermute | solution.py:546
  22.8 1.5 %collective-permute-start.4 = (bf16[2,128,384]{2,1,0:T(8,128)(2,1)S(1)}, bf16[2,128,384]{2,1,0:T(8,128)(2,1)S(1)}, u32[]{:S(2)}, u32[]{:S(2)}) collective-permute-start(bf16[2,128,384]{2,1,0:T(8,128)(2,1)S(1)} %pair_edges.1), channel_id=1, source_target_pairs={{0,32},{32,0},{64,96},{96,64},{128,160},{160,128},{192,224},{224,1... | collective-permute-start | bytes 589832 | tf_op jit(solution)/shard_map/ppermute | solution.py:595
  24.1 4.4 %copy-start = (bf16[384,1152]{1,0:T(8,128)(2,1)S(1)}, bf16[384,1152]{1,0:T(8,128)(2,1)}, u32[]{:S(2)}) copy-start(bf16[384,1152]{1,0:T(8,128)(2,1)} %weight.5) | copy-start | bytes 2654212
  25.2 10.5 %collective-permute-start.5 = (bf16[384,384]{1,0:T(8,128)(2,1)S(1)}, bf16[384,384]{1,0:T(8,128)(2,1)S(1)}, u32[]{:S(2)}, u32[]{:S(2)}) collective-permute-start(bf16[384,384]{1,0:T(8,128)(2,1)S(1)} %get-tuple-element.53.normed.refs_0_), channel_id=1, source_target_pairs={{0,1},{1,2},{2,3},{3,4},{4,5},{5,6},{6,7},{7,0},{8,9},{9,10},{10,1... | collective-permute-start | bytes 884744 | tf_op jit(solution)/shard_map/ppermute | solution.py:536
  25.2 10.4 %collective-permute-start.7 = (bf16[384,384]{1,0:T(8,128)(2,1)S(1)}, bf16[384,384]{1,0:T(8,128)(2,1)S(1)}, u32[]{:S(2)}, u32[]{:S(2)}) collective-permute-start(bf16[384,384]{1,0:T(8,128)(2,1)S(1)} %get-tuple-element.53.normed.refs_0_), channel_id=1, source_target_pairs={{0,7},{1,0},{2,1},{3,2},{4,3},{5,4},{6,5},{7,6},{8,15},{9,8},{10,9... | collective-permute-start | bytes 884744 | tf_op jit(solution)/shard_map/ppermute | solution.py:536
  29.2 11.5 %collective-permute-start.9 = (bf16[384,384]{1,0:T(8,128)(2,1)S(1)}, bf16[384,384]{1,0:T(8,128)(2,1)S(1)}, u32[]{:S(2)}, u32[]{:S(2)}) collective-permute-start(bf16[384,384]{1,0:T(8,128)(2,1)S(1)} %get-tuple-element.54.refs_5_.refs_4_), channel_id=1, source_target_pairs={{0,8},{1,9},{2,10},{3,11},{4,12},{5,13},{6,14},{7,15},{8,16},{9,17... | collective-permute-start | bytes 884744 | tf_op jit(solution)/shard_map/ppermute | solution.py:541
  29.2 11.4 %collective-permute-start.10 = (bf16[384,384]{1,0:T(8,128)(2,1)S(1)}, bf16[384,384]{1,0:T(8,128)(2,1)S(1)}, u32[]{:S(2)}, u32[]{:S(2)}) collective-permute-start(bf16[384,384]{1,0:T(8,128)(2,1)S(1)} %get-tuple-element.54.refs_5_.refs_4_), channel_id=1, source_target_pairs={{0,24},{1,25},{2,26},{3,27},{4,28},{5,29},{6,30},{7,31},{8,0},{9,1... | collective-permute-start | bytes 884744 | tf_op jit(solution)/shard_map/ppermute | solution.py:541
  35.7 9.6 %collective-permute-start.6 = (bf16[384,384]{1,0:T(8,128)(2,1)S(1)}, bf16[384,384]{1,0:T(8,128)(2,1)S(1)}, u32[]{:S(2)}, u32[]{:S(2)}) collective-permute-start(bf16[384,384]{1,0:T(8,128)(2,1)S(1)} %collective-permute-done.5.refs_1_), channel_id=1, source_target_pairs={{0,1},{1,2},{2,3},{3,4},{4,5},{5,6},{6,7},{7,0},{8,9},{9,10},{10,1... | collective-permute-start | bytes 884744 | tf_op jit(solution)/shard_map/ppermute | solution.py:536
  35.7 9.6 %collective-permute-start.8 = (bf16[384,384]{1,0:T(8,128)(2,1)S(1)}, bf16[384,384]{1,0:T(8,128)(2,1)S(1)}, u32[]{:S(2)}, u32[]{:S(2)}) collective-permute-start(bf16[384,384]{1,0:T(8,128)(2,1)S(1)} %collective-permute-done.7.refs_2_), channel_id=1, source_target_pairs={{0,7},{1,0},{2,1},{3,2},{4,3},{5,4},{6,5},{7,6},{8,15},{9,8},{10,9... | collective-permute-start | bytes 884744 | tf_op jit(solution)/shard_map/ppermute | solution.py:536
  38.9 9.6 %collective-permute-start.15 = (bf16[384,384]{1,0:T(8,128)(2,1)S(1)}, bf16[384,384]{1,0:T(8,128)(2,1)S(1)}, u32[]{:S(2)}, u32[]{:S(2)}) collective-permute-start(bf16[384,384]{1,0:T(8,128)(2,1)S(1)} %get-tuple-element.54.refs_5_.refs_4_), channel_id=1, source_target_pairs={{0,16},{1,17},{2,18},{3,19},{4,20},{5,21},{6,22},{7,23},{8,24},{9,... | collective-permute-start | bytes 884744 | tf_op jit(solution)/shard_map/ppermute | solution.py:541
  45.3 8.7 %collective-permute-start.11 = (bf16[384,384]{1,0:T(8,128)(2,1)S(1)}, bf16[384,384]{1,0:T(8,128)(2,1)S(1)}, u32[]{:S(2)}, u32[]{:S(2)}) collective-permute-start(bf16[384,384]{1,0:T(8,128)(2,1)S(1)} %get-tuple-element.56.refs_0_), channel_id=1, source_target_pairs={{0,1},{1,2},{2,3},{3,4},{4,5},{5,6},{6,7},{7,0},{8,9},{9,10},{10,1... | collective-permute-start | bytes 884744 | tf_op jit(solution)/shard_map/ppermute | solution.py:536
  45.3 8.8 %collective-permute-start.13 = (bf16[384,384]{1,0:T(8,128)(2,1)S(1)}, bf16[384,384]{1,0:T(8,128)(2,1)S(1)}, u32[]{:S(2)}, u32[]{:S(2)}) collective-permute-start(bf16[384,384]{1,0:T(8,128)(2,1)S(1)} %get-tuple-element.57.refs_1_), channel_id=1, source_target_pairs={{0,7},{1,0},{2,1},{3,2},{4,3},{5,4},{6,5},{7,6},{8,15},{9,8},{10,9... | collective-permute-start | bytes 884744 | tf_op jit(solution)/shard_map/ppermute | solution.py:536
  54.0 6.8 %collective-permute-start.12 = (bf16[192,384]{1,0:T(8,128)(2,1)S(1)}, bf16[192,384]{1,0:T(8,128)(2,1)S(1)}, u32[]{:S(2)}, u32[]{:S(2)}) collective-permute-start(bf16[192,384]{1,0:T(8,128)(2,1)S(1)} %slice.24), channel_id=1, source_target_pairs={{0,1},{1,2},{2,3},{3,4},{4,5},{5,6},{6,7},{7,0},{8,9},{9,10},{10,1... | collective-permute-start | bytes 442376 | tf_op jit(solution)/shard_map/ppermute | solution.py:536
  54.1 6.7 %collective-permute-start.14 = (bf16[192,384]{1,0:T(8,128)(2,1)S(1)}, bf16[192,384]{1,0:T(8,128)(2,1)S(1)}, u32[]{:S(2)}, u32[]{:S(2)}) collective-permute-start(bf16[192,384]{1,0:T(8,128)(2,1)S(1)} %slice.25), channel_id=1, source_target_pairs={{0,7},{1,0},{2,1},{3,2},{4,3},{5,4},{6,5},{7,6},{8,15},{9,8},{10,9... | collective-permute-start | bytes 442376 | tf_op jit(solution)/shard_map/ppermute | solution.py:536
  57.6 7.5 %copy-start.2 = (bf16[3,3,384,192]{2,3,1,0:T(8,128)(2,1)S(1)}, bf16[3,3,384,192]{2,3,1,0:T(8,128)(2,1)}, u32[]{:S(2)}) copy-start(bf16[3,3,384,192]{2,3,1,0:T(8,128)(2,1)} %param.20) | copy-start | bytes 3981316
  61.6 6.7 %collective-permute-start.16 = (bf16[208,384]{1,0:T(8,128)(2,1)S(1)}, bf16[208,384]{1,0:T(8,128)(2,1)S(1)}, u32[]{:S(2)}, u32[]{:S(2)}) collective-permute-start(bf16[208,384]{1,0:T(8,128)(2,1)S(1)} %get-tuple-element.72), channel_id=1, source_target_pairs={{0,8},{1,9},{2,10},{3,11},{4,12},{5,13},{6,14},{7,15},{8,16},{9,17... | collective-permute-start | bytes 479240 | tf_op jit(solution)/shard_map/ppermute | solution.py:541
  62.6 5.7 %collective-permute-start.17 = (bf16[208,384]{1,0:T(8,128)(2,1)S(1)}, bf16[208,384]{1,0:T(8,128)(2,1)S(1)}, u32[]{:S(2)}, u32[]{:S(2)}) collective-permute-start(bf16[208,384]{1,0:T(8,128)(2,1)S(1)} %get-tuple-element.73), channel_id=1, source_target_pairs={{0,24},{1,25},{2,26},{3,27},{4,28},{5,29},{6,30},{7,31},{8,0},{9,1... | collective-permute-start | bytes 479240 | tf_op jit(solution)/shard_map/ppermute | solution.py:541
  68.5 8.4 %copy-start.3 = (bf16[384,384]{1,0:T(8,128)(2,1)S(1)}, bf16[384,384]{1,0:T(8,128)(2,1)}, u32[]{:S(2)}) copy-start(bf16[384,384]{1,0:T(8,128)(2,1)} %wp.1) | copy-start | bytes 884740
  68.6 8.2 %collective-permute-start.18 = (bf16[400,384]{1,0:T(8,128)(2,1)S(1)}, bf16[400,384]{1,0:T(8,128)(2,1)S(1)}, u32[]{:S(2)}, u32[]{:S(2)}) collective-permute-start(bf16[400,384]{1,0:T(8,128)(2,1)S(1)} %get-tuple-element.80), channel_id=1, source_target_pairs={{0,8},{1,9},{2,10},{3,11},{4,12},{5,13},{6,14},{7,15},{8,16},{9,17... | collective-permute-start | bytes 921608 | tf_op jit(solution)/shard_map/ppermute | solution.py:541
  70.0 6.9 %collective-permute-start.19 = (bf16[400,384]{1,0:T(8,128)(2,1)S(1)}, bf16[400,384]{1,0:T(8,128)(2,1)S(1)}, u32[]{:S(2)}, u32[]{:S(2)}) collective-permute-start(bf16[400,384]{1,0:T(8,128)(2,1)S(1)} %get-tuple-element.81), channel_id=1, source_target_pairs={{0,24},{1,25},{2,26},{3,27},{4,28},{5,29},{6,30},{7,31},{8,0},{9,1... | collective-permute-start | bytes 921608 | tf_op jit(solution)/shard_map/ppermute | solution.py:541
  77.7 8.8 %collective-permute-start.20 = (bf16[1,128,384]{2,1,0:T(8,128)(2,1)S(1)}, bf16[1,128,384]{2,1,0:T(8,128)(2,1)S(1)}, u32[]{:S(2)}, u32[]{:S(2)}) collective-permute-start(bf16[1,128,384]{2,1,0:T(8,128)(2,1)S(1)} %get-tuple-element.90), channel_id=1, source_target_pairs={{0,1},{1,2},{2,3},{3,4},{4,5},{5,6},{6,7},{7,8},{8,9},{9,10},{10,1... | collective-permute-start | bytes 294920 | tf_op jit(solution)/shard_map/ppermute | solution.py:546
  77.8 8.7 %collective-permute-start.21 = (bf16[1,128,384]{2,1,0:T(8,128)(2,1)S(1)}, bf16[1,128,384]{2,1,0:T(8,128)(2,1)S(1)}, u32[]{:S(2)}, u32[]{:S(2)}) collective-permute-start(bf16[1,128,384]{2,1,0:T(8,128)(2,1)S(1)} %get-tuple-element.89), channel_id=1, source_target_pairs={{0,31},{1,0},{2,1},{3,2},{4,3},{5,4},{6,5},{7,6},{8,7},{9,8},{10,9... | collective-permute-start | bytes 294920 | tf_op jit(solution)/shard_map/ppermute | solution.py:546
